TPU v7x, 512 devices: a whole 4x8x8 slice. The times are simulated.
512 devices in a mesh: dp: 64 (over z_hi, y, core), own: 8 (over z_lo, x).
Axes of the slice: x: 4, y: 8, z: 8 (z_hi: 4, z_lo: 2; z = z_hi * 2 + z_lo), core: 2. Of those that a mesh axis runs over, the one named last changes fastest.
Arguments:
- tokens: bfloat16 [24576, 2048], P('dp'), may hold values from -6 to 6
- norm_gain: float32 [2048], replicated, may hold values from 0.5 to 1.5
- qkv_codes: bfloat16 [2048, 3, 1024], P('dp', None, 'own'), may hold values from -5 to 5
- qkv_scales: float32 [2048, 3, 8], P('dp', None, 'own'), may hold values from 0.011048543 to 0.044194173
- out_codes: bfloat16 [2048, 1024], P('dp', 'own'), may hold values from -5 to 5
- out_scales: float32 [2048, 8], P('dp', 'own'), may hold values from 0.015625 to 0.0625
- block_mask: int32 [192, 9], P('dp'), may hold values from 0 to 1, as said below
- key_counts: int32 [192], replicated, may hold values from 1 to 128, as said below
- upstream: bfloat16 [24576, 2048], P('dp'), may hold values from -0.038085938 to 0.038085938
Outputs:
- mixed: bfloat16 [24576, 2048], P('dp')
- qkv_grad: float32 [2048, 3, 1024], P('dp', None, 'own')
- out_grad: float32 [2048, 1024], P('dp', 'own')
Inputs may be any that keep to these rules, and one draw needn't show every extreme that they name: `block_mask`: the entry of a query block's own block is always 1. `key_counts`: some block is full.
All inputs are finite; a program needn't handle non-finite values.
Results may differ from a plain program's by a relative error of at most 0.035.
Values may be sent and summed in bfloat16 or wider, within the bound.
A program may use at most 64 MiB of HBM per device.

v0:
```python
import jax
import jax.numpy as jnp
from jax import lax
from jax.sharding import Mesh
from jax.sharding import PartitionSpec as P

HEAD = 128
DP = ("dp_0", "dp_1", "dp_2")


def from_everyone(x, axis):
    copies = jnp.broadcast_to(x, (lax.axis_size(axis), *x.shape))
    return lax.all_to_all(copies, axis, split_axis=0, concat_axis=0, tiled=True)


def joined_along(tiles, dim):
    shape = list(tiles.shape[1:])
    shape[dim] *= tiles.shape[0]
    return jnp.moveaxis(tiles, 0, dim).reshape(shape)


def gathered_by_axis(x, axes, dim):
    far, near = axes
    first = from_everyone(x, far)
    tiles = jnp.swapaxes(from_everyone(first, near), 0, 1)
    return joined_along(tiles.reshape(-1, *x.shape), dim)


def with_halo(cells, sides, width):
    for axis, dim in sides:
        count = lax.axis_size(axis)
        ends = count - 1
        head = lax.slice_in_dim(cells, 0, width, axis=dim)
        tail = lax.slice_in_dim(cells, cells.shape[dim] - width, cells.shape[dim], axis=dim)
        cells = jnp.concatenate(
            [
                lax.ppermute(tail, axis, [(i, (i + 1) % count) for i in range(ends)]),
                cells,
                lax.ppermute(head, axis, [((i + 1) % count, i) for i in range(ends)]),
            ],
            axis=dim,
        )
    return cells


def collect(x, axis, dim):
    tiles = from_everyone(x, axis)
    return joined_along(tiles, dim)


def from_behind(block, axis, distance):
    devices = range(lax.axis_size(axis))
    route = [(i - distance, i) for i in devices if i - distance in devices]
    return lax.ppermute(block, axis, route)


def cut_along(x, dim, length):
    shape = x.shape
    tiles = x.reshape(*shape[:dim], length, shape[dim] // length, *shape[dim + 1 :])
    return jnp.moveaxis(tiles, dim, 0)


def sent_and_summed(x, axis, dim):
    length = lax.axis_size(axis)
    tiles = lax.all_to_all(cut_along(x, dim, length), axis, 0, 0, tiled=True)
    return jnp.sum(tiles, axis=0)


def summed_rows(x, axes, dim):
    far, near = axes
    tiles = cut_along(x, dim, lax.axis_size(far))
    nearer = sent_and_summed(tiles, near, dim + 1)
    arrived = lax.all_to_all(nearer, far, split_axis=0, concat_axis=0, tiled=True)
    return arrived.sum(axis=0)


def side_by_side(arrays, axis, dim, along):
    columns = [a.reshape(*a.shape[:along], -1) for a in arrays]
    both = jnp.concatenate(columns, axis=along)
    result, at, done = (summed_rows(both, axis, dim), 0, [])
    for a, column in zip(arrays, columns):
        share = result[..., at : at + column.shape[along]]
        done.append(share.reshape(*share.shape[:along], *a.shape[along:]))
        at += column.shape[along]
    return tuple(done)


def dequant_rows(codes, scales):
    shape = codes.shape
    heads = scales.shape[-1]
    grouped = codes.astype(jnp.float32).reshape(shape[:-1] + (heads, shape[-1] // heads))
    return (grouped * scales[..., None]).reshape(shape).astype(jnp.bfloat16)


def split_heads(matrix):
    return matrix.reshape(matrix.shape[0], matrix.shape[1] // HEAD, HEAD)


def attend_forward(query_rows, key_rows, value_rows, allowed):
    inv_root = 1.0 / HEAD**0.5
    query_h = split_heads(query_rows)
    key_h = split_heads(key_rows)
    value_h = split_heads(value_rows)
    scores = (
        jnp.einsum("qhe,khe->hqk", query_h, key_h, preferred_element_type=jnp.float32) * inv_root
    )
    expo = jnp.where(allowed[None], jnp.exp(jnp.where(allowed[None], scores, 0.0)), 0.0)
    probs = expo / jnp.sum(expo, axis=-1, keepdims=True)
    probs_b = probs.astype(jnp.bfloat16)
    attended = jnp.einsum(
        "hqk,khe->qhe", probs_b, value_h, preferred_element_type=jnp.float32
    ).astype(jnp.bfloat16)
    return (attended.reshape(query_rows.shape[0], query_rows.shape[1]), probs, probs_b)


def attend_backward(query_rows, key_rows, value_rows, probs, probs_b, datt_rows):
    inv_root = 1.0 / HEAD**0.5
    query_h = split_heads(query_rows)
    key_h = split_heads(key_rows)
    value_h = split_heads(value_rows)
    datt_h = split_heads(datt_rows)
    d_prob = jnp.einsum("qhe,khe->hqk", datt_h, value_h, preferred_element_type=jnp.float32)
    delta = jnp.sum(probs * d_prob, axis=-1, keepdims=True)
    d_score = (probs * (d_prob - delta) * inv_root).astype(jnp.bfloat16)
    grad_query = jnp.einsum(
        "hqk,khe->qhe", d_score, key_h, preferred_element_type=jnp.float32
    ).astype(jnp.bfloat16)
    grad_key = jnp.einsum("hqk,qhe->khe", d_score, query_h, preferred_element_type=jnp.float32)
    grad_value = jnp.einsum("hqk,qhe->khe", probs_b, datt_h, preferred_element_type=jnp.float32)
    width = query_rows.shape[1]
    return (
        grad_query.reshape(query_rows.shape[0], width),
        grad_key.reshape(-1, width),
        grad_value.reshape(-1, width),
    )


def per_device(
    tokens,
    norm_gain,
    qkv_codes,
    qkv_scales,
    out_codes,
    out_scales,
    block_mask,
    key_counts,
    upstream,
):
    rows = tokens.shape[0]
    blocks_here = block_mask.shape[0]
    window = block_mask.shape[1]
    position = lax.axis_index(DP)
    xfloat = tokens.astype(jnp.float32)
    factor = lax.rsqrt(jnp.mean(xfloat * xfloat, axis=-1, keepdims=True) + 1e-05)
    normed = (xfloat * factor * norm_gain[None, :]).astype(jnp.bfloat16)
    full_codes, full_scales, full_out, full_out_scales = (
        gathered_by_axis(qkv_codes, (("dp_0", "dp_1"), "dp_2"), 0),
        gathered_by_axis(qkv_scales.astype(jnp.bfloat16), (("dp_0", "dp_1"), "dp_2"), 0).astype(
            qkv_scales.dtype
        ),
        gathered_by_axis(out_codes, (("dp_0", "dp_1"), "dp_2"), 0),
        gathered_by_axis(out_scales.astype(jnp.bfloat16), (("dp_0", "dp_1"), "dp_2"), 0).astype(
            out_scales.dtype
        ),
    )
    width = full_codes.shape[2]
    w_qkv = dequant_rows(full_codes, full_scales).reshape(full_codes.shape[0], 3 * width)
    w_out = dequant_rows(full_out, full_out_scales)
    qkv = (
        jnp.dot(normed, w_qkv, preferred_element_type=jnp.float32)
        .astype(jnp.bfloat16)
        .reshape(rows, 3, width)
    )
    keyval = qkv[:, 1:]
    extended = with_halo(keyval, ((DP, 0),), rows)
    zero_counts = jnp.zeros((blocks_here,), jnp.int32)
    counts_pad = jnp.concatenate([zero_counts, key_counts, zero_counts])
    counts_win = lax.dynamic_slice_in_dim(counts_pad, position * blocks_here, window, 0)
    block_len = rows // blocks_here
    within = jnp.arange(window * block_len, dtype=jnp.int32) % block_len
    live = within < jnp.repeat(counts_win, block_len)
    expanded = jnp.repeat(jnp.repeat(block_mask, block_len, axis=0), block_len, axis=1) > 0
    allowed = jnp.logical_and(expanded, live[None, :])
    d_att = jnp.dot(upstream, w_out, preferred_element_type=jnp.float32).astype(jnp.bfloat16)
    query_rows = qkv[:, 0]
    key_rows = extended[:, 0]
    value_rows = extended[:, 1]
    attended, probs, probs_b = attend_forward(query_rows, key_rows, value_rows, allowed)
    term_out = lax.dot_general(
        upstream, attended, (((0,), (0,)), ((), ())), preferred_element_type=jnp.float32
    )
    out_rows = lax.all_to_all(w_out, "own", split_axis=0, concat_axis=1, tiled=True)
    mixed_part = lax.dot_general(
        collect(attended, "own", 1),
        out_rows,
        (((1,), (1,)), ((), ())),
        preferred_element_type=jnp.float32,
    ).astype(jnp.bfloat16)
    mixed = collect(mixed_part, "own", 1)
    grad_query, grad_key, grad_value = attend_backward(
        query_rows, key_rows, value_rows, probs, probs_b, d_att
    )
    grad_keyval = jnp.stack([grad_key, grad_value], axis=1)
    from_next = from_behind(grad_keyval[:rows].astype(jnp.bfloat16), DP, -1).astype(jnp.float32)
    from_prev = from_behind(grad_keyval[2 * rows :].astype(jnp.bfloat16), DP, 1).astype(jnp.float32)
    summed_keyval = (grad_keyval[rows : 2 * rows] + from_next + from_prev).astype(jnp.bfloat16)
    d_qkv = jnp.concatenate([grad_query[:, None, :], summed_keyval], axis=1).reshape(
        rows, 3 * width
    )
    term_qkv = lax.dot_general(
        normed, d_qkv, (((0,), (0,)), ((), ())), preferred_element_type=jnp.float32
    )
    term_qkv = term_qkv.reshape(term_qkv.shape[0], 3, width)
    qkv_grad, out_grad = side_by_side((term_qkv, term_out), (("dp_0", "dp_1"), "dp_2"), 0, 1)
    return (mixed, qkv_grad, out_grad)


def solution(mesh):
    torus = Mesh(mesh.devices.reshape(4, 8, 2, mesh.shape["own"]), ("dp_0", "dp_1", "dp_2", "own"))
    placed = (
        P(DP, None),
        P(),
        P(DP, None, "own"),
        P(DP, None, "own"),
        P(DP, "own"),
        P(DP, "own"),
        P(DP, None),
        P(),
        P(DP, None),
    )
    return jax.shard_map(
        per_device,
        mesh=torus,
        in_specs=placed,
        out_specs=(P(DP, None), P(DP, None, "own"), P(DP, "own")),
        check_vma=False,
    )
```

profile of v0, /device:TPU:1, one launch (start us, length us, event | category | flops | bytes accessed | tf_op | source)
XLA Modules:
  0.0 296.4 jit_solution(3405567448313325195)
XLA Ops:
  0.7 0.8 convert_bitcast_fusion.3
  1.4 0.6 broadcast_in_dim.64
  2.1 16.5 %all-to-all-start.7 = ((bf16[32,32,1]{1,2,0:T(2,128)(2,1)}), bf16[32,32,1]{1,2,0:T(2,128)(2,1)S(1)}, u32[]{:S(2)}, u32[]{:S(2)}) async-start(bf16[32,32,1]{1,2,0:T(2,128)(2,1)} %broadcast_in_dim.64), calls=%async_computation.7 | async-start | bytes 32768 | tf_op jit(solution)/shard_map/all_to_all | solution.py:13
  18.6 0.7 broadcast_compare_fusion
  19.3 1.8 fusion.1
  21.1 0.7 convert_element_type.145
  21.9 7.7 %all-to-all-done.7 = bf16[32,32,1]{1,2,0:T(2,128)(2,1)S(1)} async-done(((bf16[32,32,1]{1,2,0:T(2,128)(2,1)}), bf16[32,32,1]{1,2,0:T(2,128)(2,1)S(1)}, u32[]{:S(2)}, u32[]{:S(2)}) %all-to-all-start.7) | async-done | bytes 2080 | tf_op jit(solution)/shard_map/all_to_all | solution.py:13
  29.5 0.6 broadcast_in_dim.55
  30.2 4.0 %all-to-all-start.2 = ((bf16[32,32,3,1]{1,2,3,0:T(4,128)(2,1)}), bf16[32,32,3,1]{1,2,3,0:T(4,128)(2,1)S(1)}, u32[]{:S(2)}, u32[]{:S(2)}) async-start(bf16[32,32,3,1]{1,2,3,0:T(4,128)(2,1)} %broadcast_in_dim.55), calls=%async_computation.2 | async-start | bytes 65536 | tf_op jit(solution)/shard_map/all_to_all | solution.py:13
  34.2 0.7 reshape.188
  34.8 10.5 %all-to-all-done.2 = bf16[32,32,3,1]{1,2,3,0:T(4,128)(2,1)S(1)} async-done(((bf16[32,32,3,1]{1,2,3,0:T(4,128)(2,1)}), bf16[32,32,3,1]{1,2,3,0:T(4,128)(2,1)S(1)}, u32[]{:S(2)}, u32[]{:S(2)}) %all-to-all-start.2) | async-done | bytes 6176 | tf_op jit(solution)/shard_map/all_to_all | solution.py:13
  45.3 6.3 %all-to-all-start.8 = ((bf16[2,2,512]{2,1,0:T(2,128)(2,1)}), bf16[2,2,512]{2,1,0:T(2,128)(2,1)S(1)}, u32[]{:S(2)}, u32[]{:S(2)}) async-start(bf16[2,2,512]{2,1,0:T(2,128)(2,1)} %reshape.188), calls=%async_computation.8 | async-start | bytes 8192 | tf_op jit(solution)/shard_map/all_to_all | solution.py:13
  51.7 0.9 all-to-all-done.8
  52.6 3.7 %all_to_all.79 = bf16[2,2,1536]{2,1,0:T(2,128)(2,1)S(1)} all-to-all(bf16[2,2,1536]{2,1,0:T(2,128)(2,1)S(1)} %reshape.186), channel_id=1, replica_groups=mesh['dp_0'=4,'dp_1'=8,'dp_2'=2,'own'=8] {'dp_2'}, dimensions={0} | all-to-all | bytes 24576 | tf_op jit(solution)/shard_map/all_to_all | solution.py:13
  56.3 0.7 broadcast_in_dim.62
  57.1 3.9 %all-to-all-start.5 = ((bf16[32,32,128]{2,1,0:T(8,128)(2,1)}), bf16[32,32,128]{2,1,0:T(8,128)(2,1)S(1)}, u32[]{:S(2)}, u32[]{:S(2)}) async-start(bf16[32,32,128]{2,1,0:T(8,128)(2,1)} %broadcast_in_dim.62), calls=%async_computation.5 | async-start | bytes 524288 | tf_op jit(solution)/shard_map/all_to_all | solution.py:13
  61.2 12.6 %all-to-all-done.5 = bf16[32,32,128]{2,1,0:T(8,128)(2,1)S(1)} async-done(((bf16[32,32,128]{2,1,0:T(8,128)(2,1)}), bf16[32,32,128]{2,1,0:T(8,128)(2,1)S(1)}, u32[]{:S(2)}, u32[]{:S(2)}) %all-to-all-start.5) | async-done | bytes 262176 | tf_op jit(solution)/shard_map/all_to_all | solution.py:13
  73.8 6.2 %all_to_all.80 = bf16[2,32,32,128]{3,2,1,0:T(8,128)(2,1)S(1)} all-to-all(bf16[2,32,32,128]{3,2,1,0:T(8,128)(2,1)S(1)} %broadcast_in_dim.63), channel_id=1, replica_groups=mesh['dp_0'=4,'dp_1'=8,'dp_2'=2,'own'=8] {'dp_2'}, dimensions={0} | all-to-all | bytes 1048576 | tf_op jit(solution)/shard_map/all_to_all | solution.py:13
  80.1 1.0 broadcast_in_dim.53
  81.1 4.1 %all-to-all-start = ((bf16[32,32,3,128]{3,1,2,0:T(8,128)(2,1)}), bf16[32,32,3,128]{3,1,2,0:T(8,128)(2,1)S(1)}, u32[]{:S(2)}, u32[]{:S(2)}) async-start(bf16[32,32,3,128]{3,1,2,0:T(8,128)(2,1)} %broadcast_in_dim.53), calls=%async_computation | async-start | bytes 1572864 | tf_op jit(solution)/shard_map/all_to_all | solution.py:13
  85.4 1.3 copy.52
  87.4 2.1 mul.79
  89.5 3.5 %copy.50 = f32[2048,384]{1,0:T(8,128)} copy(f32[2048,384]{0,1:T(8,128)} %bitcast.128) | data formatting | bytes 6291456 | tf_op jit(solution)/shard_map/mul | solution.py:92
  93.1 1.1 multiply_convert_fusion.1
  94.3 1.1 fusion.16
  95.4 11.8 %all-to-all-done = bf16[32,32,3,128]{3,1,2,0:T(8,128)(2,1)S(1)} async-done(((bf16[32,32,3,128]{3,1,2,0:T(8,128)(2,1)}), bf16[32,32,3,128]{3,1,2,0:T(8,128)(2,1)S(1)}, u32[]{:S(2)}, u32[]{:S(2)}) %all-to-all-start) | async-done | bytes 786464 | tf_op jit(solution)/shard_map/all_to_all | solution.py:13
  107.4 7.5 %all_to_all.81 = bf16[2,32,32,3,128]{4,2,3,1,0:T(8,128)(2,1)S(1)} all-to-all(bf16[2,32,32,3,128]{4,2,3,1,0:T(8,128)(2,1)S(1)} %broadcast_in_dim.54), channel_id=1, replica_groups=mesh['dp_0'=4,'dp_1'=8,'dp_2'=2,'own'=8] {'dp_2'}, dimensions={0} | all-to-all | bytes 3145728 | tf_op jit(solution)/shard_map/all_to_all | solution.py:13
  115.0 5.6 %all-to-all-start.9 = ((bf16[8,256,128]{2,1,0:T(8,128)(2,1)}), bf16[8,256,128]{2,1,0:T(8,128)(2,1)}, u32[]{:S(2)}, u32[]{:S(2)}) async-start(bf16[8,256,128]{2,1,0:T(8,128)(2,1)} %multiply_convert_fusion.1), calls=%async_computation.9 | async-start | bytes 1048576 | tf_op jit(solution)/shard_map/all_to_all | solution.py:192
  121.0 3.0 copy.47
  124.0 1.2 fusion.9
  125.3 2.7 collective-permute-start.1
  128.0 4.4 %collective-permute-start = (bf16[384,2,128]{0,2,1:T(8,128)(2,1)S(1)}, bf16[384,2,128]{0,2,1:T(8,128)(2,1)S(1)}, u32[]{:S(2)}, u32[]{:S(2)}) collective-permute-start(bf16[384,2,128]{0,2,1:T(8,128)(2,1)S(1)} %slice.38), channel_id=1, source_target_pairs={{0,8},{8,16},{16,24},{24,32},{32,40},{40,48},{48,56},{56,64},{64,7... | collective-permute-start | bytes 589832 | tf_op jit(solution)/shard_map/ppermute | solution.py:37
  132.4 1.3 convolution_convert_fusion.2
  133.6 1.1 collective-permute-done
  134.8 0.8 fusion.34
  135.6 1.2 copy-done.11
  136.8 1.1 fusion.14
  138.0 1.0 copy.53
  139.0 2.3 multiply_reduce_fusion
  143.1 0.8 copy-done.8
  143.8 0.8 fusion.33
  144.6 4.4 %collective-permute-start.3 = (bf16[384,2,128]{0,2,1:T(8,128)(2,1)}, bf16[384,2,128]{0,2,1:T(8,128)(2,1)S(1)}, u32[]{:S(2)}, u32[]{:S(2)}) collective-permute-start(bf16[384,2,128]{0,2,1:T(8,128)(2,1)} %get-tuple-element.16), channel_id=1, source_target_pairs={{0,8},{8,16},{16,24},{24,32},{32,40},{40,48},{48,56},{56,64},{64,7... | collective-permute-start | bytes 589832 | tf_op jit(solution)/shard_map/ppermute | solution.py:54
  149.0 1.9 collective-permute-start.2
  151.0 1.0 broadcast_in_dim.61
  151.9 5.4 %all-to-all-start.4 = ((bf16[8,384,128]{2,1,0:T(8,128)(2,1)}), bf16[8,384,128]{2,1,0:T(8,128)(2,1)}, u32[]{:S(2)}, u32[]{:S(2)}) async-start(bf16[8,384,128]{2,1,0:T(8,128)(2,1)} %broadcast_in_dim.61), calls=%async_computation.4 | async-start | bytes 1572864 | tf_op jit(solution)/shard_map/all_to_all | solution.py:13
  157.8 0.7 copy-done.5
  159.1 1.0 fusion.27
  160.2 1.1 fusion.19
  161.3 2.2 pad_maximum_fusion
  163.5 5.4 %copy.58 = f32[2048,512]{1,0:T(8,128)} copy(f32[2048,512]{0,1:T(8,128)} %pad_maximum_fusion) | data formatting | bytes 8388608 | tf_op jit(solution)/shard_map/concatenate | solution.py:79
  169.0 5.0 %copy.59 = f32[2,32,32,512]{3,2,1,0:T(8,128)} copy(f32[2,32,32,512]{3,2,0,1:T(8,128)} %bitcast.126) | data formatting | bytes 8388608 | tf_op jit(solution)/shard_map/transpose | solution.py:60
  173.9 5.7 %all-to-all-start.11 = ((f32[2,32,32,512]{3,2,1,0:T(8,128)}), f32[2,32,32,512]{3,2,1,0:T(8,128)}, u32[]{:S(2)}, u32[]{:S(2)}) async-start(f32[2,32,32,512]{3,2,1,0:T(8,128)} %copy.59), calls=%async_computation.11 | async-start | bytes 8388608 | tf_op jit(solution)/shard_map/all_to_all | solution.py:65
  179.6 1.7 fusion.13
  181.3 2.4 all-to-all-done.11
  183.7 1.2 broadcast_in_dim.66
  184.9 5.1 %all-to-all-start.10 = ((bf16[8,384,256]{2,1,0:T(8,128)(2,1)}), bf16[8,384,256]{2,1,0:T(8,128)(2,1)S(1)}, u32[]{:S(2)}, u32[]{:S(2)}) async-start(bf16[8,384,256]{2,1,0:T(8,128)(2,1)} %broadcast_in_dim.66), calls=%async_computation.10 | async-start | bytes 3145728 | tf_op jit(solution)/shard_map/all_to_all | solution.py:13
  190.1 4.2 %reduce_sum.48 = f32[32,32,512]{2,1,0:T(8,128)} reduce(f32[2,32,32,512]{3,2,1,0:T(8,128)} %all-to-all-done.11, f32[]{:T(128)} %constant.16.clone.1), dimensions={0}, to_apply=%region_3.4 | reduce | flops 524288 | bytes 6291460 | tf_op jit(solution)/shard_map/reduce_sum | solution.py:66
  194.3 16.3 %all-to-all-done.10 = bf16[8,384,256]{2,1,0:T(8,128)(2,1)S(1)} async-done(((bf16[8,384,256]{2,1,0:T(8,128)(2,1)}), bf16[8,384,256]{2,1,0:T(8,128)(2,1)S(1)}, u32[]{:S(2)}, u32[]{:S(2)}) %all-to-all-start.10) | async-done | bytes 1572896 | tf_op jit(solution)/shard_map/all_to_all | solution.py:13
  210.7 16.0 %all-to-all-start.12 = ((f32[32,32,512]{2,1,0:T(8,128)}), f32[32,32,512]{2,1,0:T(8,128)}, u32[]{:S(2)}, u32[]{:S(2)}) async-start(f32[32,32,512]{2,1,0:T(8,128)} %reduce_sum.48), calls=%async_computation.12 | async-start | bytes 4194304 | tf_op jit(solution)/shard_map/all_to_all | solution.py:73
  226.7 0.9 copy.56
  227.5 1.6 copy.60
  229.2 64.3 %all-to-all-done.12 = f32[32,32,512]{2,1,0:T(8,128)} async-done(((f32[32,32,512]{2,1,0:T(8,128)}), f32[32,32,512]{2,1,0:T(8,128)}, u32[]{:S(2)}, u32[]{:S(2)}) %all-to-all-start.12) | async-done | bytes 2097184 | tf_op jit(solution)/shard_map/all_to_all | solution.py:73
  293.5 1.7 reduce_sum.49
  295.2 0.6 copy_bitcast_fusion
  (85 shorter events, 5.8 us)
Async XLA Ops:
  0.6 131.7 %copy-start = (bf16[384,2048]{1,0:T(8,128)(2,1)S(1)}, bf16[384,2048]{1,0:T(8,128)(2,1)}, u32[]{:S(2)}) copy-start(bf16[384,2048]{1,0:T(8,128)(2,1)} %param.17) | copy-start | bytes 4718596
  0.6 55.7 %copy-start.20 = (bf16[32,128]{1,0:T(8,128)(2,1)S(1)}, bf16[32,128]{1,0:T(8,128)(2,1)}, u32[]{:S(2)}) copy-start(bf16[32,128]{1,0:T(8,128)(2,1)} %param.13) | copy-start | bytes 24580
  0.7 60.3 %copy-start.21 = (s32[192]{0:T(256)S(1)}, s32[192]{0:T(256)}, u32[]{:S(2)}) copy-start(s32[192]{0:T(256)} %param.16) | copy-start | bytes 2308
  2.1 27.5 %all-to-all-start.7 = ((bf16[32,32,1]{1,2,0:T(2,128)(2,1)}), bf16[32,32,1]{1,2,0:T(2,128)(2,1)S(1)}, u32[]{:S(2)}, u32[]{:S(2)}) async-start(bf16[32,32,1]{1,2,0:T(2,128)(2,1)} %broadcast_in_dim.64), calls=%async_computation.7 | async-start | bytes 32768 | tf_op jit(solution)/shard_map/all_to_all | solution.py:13
  21.1 59.0 %copy-start.19 = (bf16[32,3,128]{2,0,1:T(8,128)(2,1)S(1)}, bf16[32,3,128]{2,0,1:T(8,128)(2,1)}, u32[]{:S(2)}) copy-start(bf16[32,3,128]{2,0,1:T(8,128)(2,1)} %param.11) | copy-start | bytes 73732
  30.2 15.1 %all-to-all-start.2 = ((bf16[32,32,3,1]{1,2,3,0:T(4,128)(2,1)}), bf16[32,32,3,1]{1,2,3,0:T(4,128)(2,1)S(1)}, u32[]{:S(2)}, u32[]{:S(2)}) async-start(bf16[32,32,3,1]{1,2,3,0:T(4,128)(2,1)} %broadcast_in_dim.55), calls=%async_computation.2 | async-start | bytes 65536 | tf_op jit(solution)/shard_map/all_to_all | solution.py:13
  45.3 7.3 %all-to-all-start.8 = ((bf16[2,2,512]{2,1,0:T(2,128)(2,1)}), bf16[2,2,512]{2,1,0:T(2,128)(2,1)S(1)}, u32[]{:S(2)}, u32[]{:S(2)}) async-start(bf16[2,2,512]{2,1,0:T(2,128)(2,1)} %reshape.188), calls=%async_computation.8 | async-start | bytes 8192 | tf_op jit(solution)/shard_map/all_to_all | solution.py:13
  57.1 16.7 %all-to-all-start.5 = ((bf16[32,32,128]{2,1,0:T(8,128)(2,1)}), bf16[32,32,128]{2,1,0:T(8,128)(2,1)S(1)}, u32[]{:S(2)}, u32[]{:S(2)}) async-start(bf16[32,32,128]{2,1,0:T(8,128)(2,1)} %broadcast_in_dim.62), calls=%async_computation.5 | async-start | bytes 524288 | tf_op jit(solution)/shard_map/all_to_all | solution.py:13
  81.1 26.2 %all-to-all-start = ((bf16[32,32,3,128]{3,1,2,0:T(8,128)(2,1)}), bf16[32,32,3,128]{3,1,2,0:T(8,128)(2,1)S(1)}, u32[]{:S(2)}, u32[]{:S(2)}) async-start(bf16[32,32,3,128]{3,1,2,0:T(8,128)(2,1)} %broadcast_in_dim.53), calls=%async_computation | async-start | bytes 1572864 | tf_op jit(solution)/shard_map/all_to_all | solution.py:13
  115.0 36.0 %all-to-all-start.9 = ((bf16[8,256,128]{2,1,0:T(8,128)(2,1)}), bf16[8,256,128]{2,1,0:T(8,128)(2,1)}, u32[]{:S(2)}, u32[]{:S(2)}) async-start(bf16[8,256,128]{2,1,0:T(8,128)(2,1)} %multiply_convert_fusion.1), calls=%async_computation.9 | async-start | bytes 1048576 | tf_op jit(solution)/shard_map/all_to_all | solution.py:192
  121.0 3.0 %copy-start.2 = (bf16[384,2048]{1,0:T(8,128)(2,1)S(1)}, bf16[384,2048]{1,0:T(8,128)(2,1)}, u32[]{:S(2)}) copy-start(bf16[384,2048]{1,0:T(8,128)(2,1)} %param.9) | copy-start | bytes 4718596
  121.0 3.0 %copy-start.3 = (f32[2048,384]{1,0:T(8,128)S(1)}, f32[2048,384]{1,0:T(8,128)}, u32[]{:S(2)}) copy-start(f32[2048,384]{1,0:T(8,128)} %copy.50) | copy-start | bytes 9437188
  121.0 3.0 %copy-start.18 = (f32[2048]{0:T(1024)S(1)}, f32[2048]{0:T(1024)}, u32[]{:S(2)}) copy-start(f32[2048]{0:T(1024)} %param.10) | copy-start | bytes 24580
  124.0 8.4 %copy-start.10 = (bf16[2048,128]{1,0:T(8,128)(2,1)S(1)}, bf16[2048,128]{1,0:T(8,128)(2,1)}, u32[]{:S(2)}) copy-start(bf16[2048,128]{1,0:T(8,128)(2,1)} %fusion.16) | copy-start | bytes 1572868
  125.2 9.6 %copy-start.15 = (pred[384,1152]{1,0:T(32,128)(4,1)S(1)}, pred[384,1152]{1,0:T(32,128)(4,1)}, u32[]{:S(2)}) copy-start(pred[384,1152]{1,0:T(32,128)(4,1)} %copy.52) | copy-start | bytes 1327108
  125.3 8.4 %collective-permute-start.1 = (bf16[384,2,128]{0,2,1:T(8,128)(2,1)S(1)}, bf16[384,2,128]{0,2,1:T(8,128)(2,1)S(1)}, u32[]{:S(2)}, u32[]{:S(2)}) collective-permute-start(bf16[384,2,128]{0,2,1:T(8,128)(2,1)S(1)} %slice.38), channel_id=1, source_target_pairs={{8,0},{16,8},{24,16},{32,24},{40,32},{48,40},{56,48},{64,56},{72,6... | collective-permute-start | bytes 589832 | tf_op jit(solution)/shard_map/ppermute | solution.py:39
  128.0 6.8 %collective-permute-start = (bf16[384,2,128]{0,2,1:T(8,128)(2,1)S(1)}, bf16[384,2,128]{0,2,1:T(8,128)(2,1)S(1)}, u32[]{:S(2)}, u32[]{:S(2)}) collective-permute-start(bf16[384,2,128]{0,2,1:T(8,128)(2,1)S(1)} %slice.38), channel_id=1, source_target_pairs={{0,8},{8,16},{16,24},{24,32},{32,40},{40,48},{48,56},{56,64},{64,7... | collective-permute-start | bytes 589832 | tf_op jit(solution)/shard_map/ppermute | solution.py:37
  134.8 0.8 copy-start.13
  135.6 1.2 copy-start.11
  139.0 2.3 copy-start.12
  141.3 0.9 copy-start.17
  141.6 0.9 copy-start.4
  142.2 0.8 copy-start.6
  143.0 0.9 copy-start.8
  143.8 13.5 %copy-start.16 = (bf16[384,128]{0,1:T(8,128)(2,1)S(1)}, bf16[384,128]{0,1:T(8,128)(2,1)}, u32[]{:S(2)}) copy-start(bf16[384,128]{0,1:T(8,128)(2,1)} %fusion.14) | copy-start | bytes 294916
  144.6 14.5 %collective-permute-start.3 = (bf16[384,2,128]{0,2,1:T(8,128)(2,1)}, bf16[384,2,128]{0,2,1:T(8,128)(2,1)S(1)}, u32[]{:S(2)}, u32[]{:S(2)}) collective-permute-start(bf16[384,2,128]{0,2,1:T(8,128)(2,1)} %get-tuple-element.16), channel_id=1, source_target_pairs={{0,8},{8,16},{16,24},{24,32},{32,40},{40,48},{48,56},{56,64},{64,7... | collective-permute-start | bytes 589832 | tf_op jit(solution)/shard_map/ppermute | solution.py:54
  149.0 10.1 %collective-permute-start.2 = (bf16[384,2,128]{0,2,1:T(8,128)(2,1)}, bf16[384,2,128]{0,2,1:T(8,128)(2,1)}, u32[]{:S(2)}, u32[]{:S(2)}) collective-permute-start(bf16[384,2,128]{0,2,1:T(8,128)(2,1)} %get-tuple-element.15), channel_id=1, source_target_pairs={{8,0},{16,8},{24,16},{32,24},{40,32},{48,40},{56,48},{64,56},{72,6... | collective-permute-start | bytes 589832 | tf_op jit(solution)/shard_map/ppermute | solution.py:54
  151.9 22.0 %all-to-all-start.4 = ((bf16[8,384,128]{2,1,0:T(8,128)(2,1)}), bf16[8,384,128]{2,1,0:T(8,128)(2,1)}, u32[]{:S(2)}, u32[]{:S(2)}) async-start(bf16[8,384,128]{2,1,0:T(8,128)(2,1)} %broadcast_in_dim.61), calls=%async_computation.4 | async-start | bytes 1572864 | tf_op jit(solution)/shard_map/all_to_all | solution.py:13
  157.4 1.2 copy-start.5
  157.4 1.3 copy-start.14
  157.4 1.7 copy-start.7
  157.4 1.7 copy-start.9
  173.9 9.8 %all-to-all-start.11 = ((f32[2,32,32,512]{3,2,1,0:T(8,128)}), f32[2,32,32,512]{3,2,1,0:T(8,128)}, u32[]{:S(2)}, u32[]{:S(2)}) async-start(f32[2,32,32,512]{3,2,1,0:T(8,128)} %copy.59), calls=%async_computation.11 | async-start | bytes 8388608 | tf_op jit(solution)/shard_map/all_to_all | solution.py:65
  184.9 25.7 %all-to-all-start.10 = ((bf16[8,384,256]{2,1,0:T(8,128)(2,1)}), bf16[8,384,256]{2,1,0:T(8,128)(2,1)S(1)}, u32[]{:S(2)}, u32[]{:S(2)}) async-start(bf16[8,384,256]{2,1,0:T(8,128)(2,1)} %broadcast_in_dim.66), calls=%async_computation.10 | async-start | bytes 3145728 | tf_op jit(solution)/shard_map/all_to_all | solution.py:13
  210.7 82.8 %all-to-all-start.12 = ((f32[32,32,512]{2,1,0:T(8,128)}), f32[32,32,512]{2,1,0:T(8,128)}, u32[]{:S(2)}, u32[]{:S(2)}) async-start(f32[32,32,512]{2,1,0:T(8,128)} %reduce_sum.48), calls=%async_computation.12 | async-start | bytes 4194304 | tf_op jit(solution)/shard_map/all_to_all | solution.py:73
  227.5 68.9 %copy-start.1 = (bf16[384,2048]{1,0:T(8,128)(2,1)S(1)}, bf16[384,2048]{1,0:T(8,128)(2,1)}, u32[]{:S(2)}) copy-start(bf16[384,2048]{1,0:T(8,128)(2,1)} %param.17) | copy-start | bytes 4718596
where the time goes:
time: 300 us; the launch traced here: 296 us
  waiting for transfers between devices  128 us (43%)
  starting transfers between devices  85.8 us (29%)
  local copies, waits for them, and re-layouts  36.6 us (12%)
  blocking collectives  17.4 us (6%)
  other arithmetic  16.7 us (6%)
  matrix products  11 us (4%)
    all_to_all x1, waiting for transfers between devices, summed_rows(): lax.all_to_all(nearer, far, split_axis=0, concat_axis=0, tiled=True)  64.3 us
    all_to_all x7, waiting for transfers between devices, from_everyone(): return lax.all_to_all(copies, axis, split_axis=0, concat_axis=0, tiled=True)  59.8 us
    all_to_all x7, starting transfers between devices, from_everyone(): return lax.all_to_all(copies, axis, split_axis=0, concat_axis=0, tiled=True)  45.3 us
    all_to_all x3, blocking collectives, from_everyone(): return lax.all_to_all(copies, axis, split_axis=0, concat_axis=0, tiled=True)  17.4 us
    all_to_all x1, starting transfers between devices, summed_rows(): lax.all_to_all(nearer, far, split_axis=0, concat_axis=0, tiled=True)  16 us
    unnamed x57, local copies, waits for them, and re-layouts  6.82 us
    ppermute x2, starting transfers between devices, from_behind(): return lax.ppermute(block, axis, route)  6.29 us
  transfers between devices with their start and end apart: 14, of which 9 were waited for; matrix products, arithmetic and copies ran while one was open for 18% of the time, Pallas kernels for 0%

commit v1 on v0

v1 whole, which is shorter than its diff:
```python
import functools
import math

import jax
import jax.numpy as jnp
from jax import lax
from jax.experimental import pallas as pl
from jax.experimental.pallas import tpu as pltpu
from jax.sharding import Mesh
from jax.sharding import PartitionSpec as P

HEAD = 128
BLK = 128
ROWS = 32
COLS = 4 * HEAD
AXES = ("zh", "y", "core", "zl", "x")
DP = ("zh", "y", "core")
OWN = ("zl", "x")
BF = jnp.bfloat16
F32 = jnp.float32
MESH = pl.DeviceIdType.MESH
INV_ROOT = 1.0 / HEAD**0.5
TO_EXP2 = INV_ROOT * math.log2(math.e)


def nn(a, b):
    return lax.dot_general(a, b, (((1,), (0,)), ((), ())), preferred_element_type=F32)


def nt(a, b):
    return lax.dot_general(a, b, (((1,), (1,)), ((), ())), preferred_element_type=F32)


def tn(a, b):
    return lax.dot_general(a, b, (((0,), (0,)), ((), ())), preferred_element_type=F32)


def kernel(
    dims,
    tok, gain, wblk, bias, ups,
    mixed, gq, go,
    normed, ntr, utr, nts, uts, wbuf, qd, kv, ebuf, pbuf, dsb, dqa, atts, att_all, wo, mxs,
    hgs, hgr, ogr, dd, g, rss, rsr, zs, zr,
    agz, agy, ags, halo, tsw, wos, ats, hgm, dds, rsm, zsm, mxm, loc,
):
    ZH, Y, ZL, X = dims
    H = Y // 2
    NOWN = ZL * X
    T, D = tok.shape
    NQ = T // BLK
    share = D // NOWN
    ny = ZH * Y // NOWN
    zh, y, c = lax.axis_index("zh"), lax.axis_index("y"), lax.axis_index("core")
    own = lax.axis_index("zl") * X + lax.axis_index("x")
    sib = {"core": 1 - c}
    pending = []

    def rcopy(src, dst, sems, index, dev):
        return pltpu.make_async_remote_copy(
            src_ref=src,
            dst_ref=dst,
            send_sem=sems.at[(0, *index)],
            recv_sem=sems.at[(1, *index)],
            device_id=dev,
            device_id_type=MESH,
        )

    def send(src, dst, sems, index, dev):
        cp = rcopy(src, dst, sems, index, dev)
        cp.start()
        pending.append(cp)

    def arrived(dst, sems, index, dev):
        rcopy(dst, dst, sems, index, dev).wait_recv()

    def zk(k):
        return lax.rem(zh + k, ZH)

    def yd(d):
        return lax.rem(y + (d + Y), Y)

    def ydev(d):
        return {"y": yd(d)}

    def owner(j):
        return lax.rem(own + j, NOWN)

    def odev(o):
        return {"zl": o // X, "x": lax.rem(o, X)}

    def half(d, k):
        return (k < ZH // 2) == (d == 0)

    place = (zh * Y + y) * 2 + c
    count = ZH * Y * 2

    def range_dev(step):
        r = lax.rem(place + step + count, count)
        return {"zh": r // (2 * Y), "y": lax.rem(r // 2, Y), "core": lax.rem(r, 2)}

    nxt, prv = range_dev(1), range_dev(-1)

    barrier = pltpu.get_barrier_semaphore()
    partners = [sib, ydev(1), ydev(-1), nxt, prv]
    partners += [{"zh": zk(k)} for k in range(1, ZH)]
    partners += [odev(owner(j)) for j in range(1, NOWN)]
    for dev in partners:
        pl.semaphore_signal(barrier, inc=1, device_id=dev, device_id_type=MESH)
    wbuf[zh, y, c] = wblk[...]
    pl.semaphore_wait(barrier, len(partners))

    def block(k, d):
        return wbuf.at[zk(k), yd(d), c]

    def ag_send(d, h, k):
        s = 1 if d == 0 else -1
        b = block(k, -s * (h - 1))
        send(b, b, agy, (d, h - 1, k), ydev(s))

    def ag_wait(d, h, k):
        s = 1 if d == 0 else -1
        arrived(block(k, -s * h), agy, (d, h - 1, k), ydev(s))

    def ag_pass(dy):
        b = wbuf.at[:, yd(dy), c]
        send(b, b, ags, (dy % Y,), sib)

    mine = wbuf.at[zh, y, c]
    ag_send(0, 1, 0)
    ag_send(1, 1, 0)
    for k in range(1, ZH):
        send(mine, mine, agz, (k,), {"zh": zk(k)})

    def norm_rows(i, carry):
        r = pl.ds(pl.multiple_of(i * 16, 16), 16)
        x = tok[r, :].astype(F32)
        factor = lax.rsqrt(jnp.mean(x * x, axis=-1, keepdims=True) + 1e-05)
        normed[r, :] = (x * factor * gain[...]).astype(BF)
        return carry

    def turn(src, dst):
        per = Y // 2

        def body(j, carry):
            v = src[:, pl.ds(pl.multiple_of(j * 128, 128), 128)]
            dst[j // per, pl.ds(2 * lax.rem(j, per), 2)] = v.T.reshape(2, 2, ROWS, T)
            return carry

        return body

    lax.fori_loop(0, T // 16, norm_rows, 0)
    for k in range(1, ZH):
        arrived(wbuf.at[zk(ZH - k), y, c], agz, (k,), sib)
    for k in range(1, ZH):
        ag_send(0, 1, k)
        ag_send(1, 1, k)
    ag_pass(0)

    def fill(h):
        if h == 1:
            lax.fori_loop(0, D // 128, turn(ups, utr), 0)
            send(utr.at[:, :, 1 - c], uts, tsw, (0,), sib)
        if h == 2:
            lax.fori_loop(0, D // 128, turn(normed, ntr), 0)
            send(ntr.at[:, :, 1 - c], nts, tsw, (1,), sib)

    for h in range(1, H + 1):
        for k in range(ZH):
            for d in (0, 1):
                if h == H and not half(d, k):
                    continue
                ag_wait(d, h, k)
                if h < H - 1 or (h == H - 1 and half(d, k)):
                    ag_send(d, h + 1, k)
        ag_pass(-h)
        if h < H:
            ag_pass(h)
        fill(h)
    for dy in range(Y):
        arrived(wbuf.at[:, yd(dy), 1 - c], ags, (dy,), sib)

    def project(src, lo, n):
        total = None
        for z in range(ZH):
            w = wbuf[z, :, :, :, lo : lo + n].reshape(Y * 2 * ROWS, n)
            term = nn(src[:, z * Y * 64 : (z + 1) * Y * 64], w)
            total = term if total is None else total + term
        return total.astype(BF)

    keyval = project(normed, HEAD, 2 * HEAD)
    kv[1, 0] = keyval[:, :HEAD]
    kv[1, 1] = keyval[:, HEAD:]
    for j in range(2):
        send(kv.at[1, j], kv.at[0, j], halo, (0, j), nxt)
        send(kv.at[1, j], kv.at[2, j], halo, (1, j), prv)
    qd[0] = project(normed, 0, HEAD)
    qd[1] = project(ups, 3 * HEAD, HEAD)

    def wo_part(o):
        at = o * ny
        return wbuf.at[at // Y, pl.ds(lax.rem(at, Y), ny), :, :, pl.ds(3 * HEAD, HEAD)]

    def lanes(o, n):
        return pl.ds(pl.multiple_of(o * n, n), n)

    for j in range(1, NOWN):
        o = owner(j)
        send(wo_part(o), wo.at[:, :, :, lanes(own, HEAD)], wos, (j,), odev(o))
    keep_wo = pltpu.make_async_copy(wo_part(own), wo.at[:, :, :, lanes(own, HEAD)], loc.at[0])
    keep_wo.start()

    sums = [None] * NQ
    for seg in (1, 0, 2):
        if seg != 1:
            arrived(kv.at[seg, 0], halo, (seg // 2, 0), sib)
        for b in range(NQ):
            rows = slice(b * BLK, (b + 1) * BLK)
            score = nt(qd[0, rows, :], kv[seg, 0])
            e = jnp.exp2(score * TO_EXP2 + bias[b * 3 + seg : b * 3 + seg + 1, :])
            ebuf[seg, rows, :] = e
            part = jnp.sum(e, axis=-1, keepdims=True)
            sums[b] = part if sums[b] is None else sums[b] + part
    for seg in (0, 2):
        arrived(kv.at[seg, 1], halo, (seg // 2, 1), sib)
    deltas = []
    for b in range(NQ):
        rows = slice(b * BLK, (b + 1) * BLK)
        scale = 1.0 / sums[b]
        total = None
        for seg in range(3):
            p = ebuf[seg, rows, :] * scale
            ebuf[seg, rows, :] = p
            pb = p.astype(BF)
            pbuf[seg, rows, :] = pb
            term = nn(pb, kv[seg, 1])
            total = term if total is None else total + term
        atts[rows, :] = total.astype(BF)
        deltas.append(jnp.sum(total * qd[1, rows, :].astype(F32), axis=-1, keepdims=True))
    for j in range(1, NOWN):
        o = owner(j)
        send(atts, att_all.at[:, lanes(own, HEAD)], ats, (j,), odev(o))
    keep_att = pltpu.make_async_copy(atts, att_all.at[:, lanes(own, HEAD)], loc.at[1])
    keep_att.start()
    dd[0, :, 3 * HEAD :] = atts[...]
    send(dd.at[0, :, pl.ds(3 * HEAD, HEAD)], dd.at[1, :, pl.ds(3 * HEAD, HEAD)], dds, (0,), sib)

    for seg in (0, 2, 1):
        for b in range(NQ):
            rows = slice(b * BLK, (b + 1) * BLK)
            dp = nt(qd[1, rows, :], kv[seg, 1])
            ds = (ebuf[seg, rows, :] * (dp - deltas[b]) * INV_ROOT).astype(BF)
            dsb[seg, rows, :] = ds
            term = nn(ds, kv[seg, 0])
            if seg == 0:
                dqa[rows, :] = term
            else:
                dqa[rows, :] += term
        dk = tn(dsb[seg], qd[0])
        dv = tn(pbuf[seg], qd[1])
        if seg == 1:
            ogr[0] = dk
            ogr[1] = dv
        else:
            hgs[seg // 2, 0] = dk.astype(BF)
            hgs[seg // 2, 1] = dv.astype(BF)
            send(hgs.at[seg // 2], hgr.at[seg // 2], hgm, (seg // 2,), prv if seg == 0 else nxt)
    dd[0, :, :HEAD] = dqa[...].astype(BF)
    for side in range(2):
        arrived(hgr.at[side], hgm, (side,), sib)
    for j in range(2):
        both = ogr[j] + hgr[0, j].astype(F32) + hgr[1, j].astype(F32)
        dd[0, :, (j + 1) * HEAD : (j + 2) * HEAD] = both.astype(BF)
    send(dd.at[0, :, pl.ds(0, 3 * HEAD)], dd.at[1, :, pl.ds(0, 3 * HEAD)], dds, (1,), sib)
    arrived(uts, tsw, (0,), sib)
    arrived(nts, tsw, (1,), sib)
    arrived(dd.at[1, :, pl.ds(3 * HEAD, HEAD)], dds, (0,), sib)
    arrived(dd.at[1, :, pl.ds(0, 3 * HEAD)], dds, (1,), sib)

    def term_at(dy):
        yy = yd(dy)
        high = ZH * ROWS
        a = nn(ntr[:, yy, c].reshape(high, T), dd[0, :, : 3 * HEAD])
        a += nn(nts[:, yy].reshape(high, T), dd[1, :, : 3 * HEAD])
        b = nn(utr[:, yy, c].reshape(high, T), dd[0, :, 3 * HEAD :])
        b += nn(uts[:, yy].reshape(high, T), dd[1, :, 3 * HEAD :])
        g[dy % Y, :, :, : 3 * HEAD] = a.reshape(ZH, ROWS, 3 * HEAD)
        g[dy % Y, :, :, 3 * HEAD :] = b.reshape(ZH, ROWS, HEAD)

    def rs_wait(d, t, k):
        arrived(rsr.at[d, t, k], rsm, (d, t, k), sib)

    def mix():
        keep_wo.wait()
        keep_att.wait()
        for j in range(1, NOWN):
            o = owner(NOWN - j)
            arrived(wo.at[:, :, :, lanes(o, HEAD)], wos, (j,), sib)
            arrived(att_all.at[:, lanes(o, HEAD)], ats, (j,), sib)
        w = wo[...].reshape(share, NOWN * HEAD)
        for b in range(NQ):
            rows = slice(b * BLK, (b + 1) * BLK)
            mxs[rows, :] = nt(att_all[rows, :], w).astype(BF)
        for j in range(1, NOWN):
            send(mxs, mixed.at[:, lanes(own, share)], mxm, (j,), odev(owner(j)))

    order = [*range(1, ZH), 0]
    for t in range(H):
        term_at(H - t)
        if t > 0:
            term_at(t - H)
        if t == H - 1:
            term_at(0)
        for k in order:
            for d in (0, 1):
                s = 1 if d == 0 else -1
                if t == 0 and not half(d, k):
                    continue
                val = g[(s * (H - t)) % Y, zk(k)]
                if t > 1 or (t == 1 and half(d, k)):
                    rs_wait(d, t - 1, k)
                    val += rsr[d, t - 1, k].astype(F32)
                rss[d, t, k] = val.astype(BF)
                send(rss.at[d, t, k], rsr.at[d, t, k], rsm, (d, t, k), ydev(s))
        if t == 1:
            mix()
    kept = None
    for k in order:
        val = g[0, zk(k)]
        for d in (0, 1):
            rs_wait(d, H - 1, k)
            val += rsr[d, H - 1, k].astype(F32)
        if k:
            zs[k] = val.astype(BF)
            send(zs.at[k], zr.at[k], zsm, (k,), {"zh": zk(k)})
        else:
            kept = val
    for k in range(1, ZH):
        arrived(zr.at[k], zsm, (k,), sib)
        kept += zr[k].astype(F32)
    gq[...] = kept[:, : 3 * HEAD]
    go[...] = kept[:, 3 * HEAD :]

    keep_mix = pltpu.make_async_copy(mxs, mixed.at[:, lanes(own, share)], loc.at[2])
    keep_mix.start()
    keep_mix.wait()
    for j in range(1, NOWN):
        arrived(mixed.at[:, lanes(owner(NOWN - j), share)], mxm, (j,), sib)
    for cp in pending:
        cp.wait_send()


def per_device(
    dims,
    tokens, norm_gain, qkv_codes, qkv_scales, out_codes, out_scales, block_mask, key_counts, upstream,
):
    ZH, Y, ZL, X = dims
    H = Y // 2
    NOWN = ZL * X
    T, D = tokens.shape
    place = lax.axis_index(DP)
    blocks = block_mask.shape[0]
    window = block_mask.shape[1]
    w_qkv = (qkv_codes.astype(F32) * qkv_scales).reshape(ROWS, 3 * HEAD)
    w_out = out_codes.astype(F32) * out_scales
    wblk = jnp.concatenate([w_qkv, w_out], axis=1).astype(BF)
    pad = jnp.zeros((blocks,), jnp.int32)
    counts = lax.dynamic_slice_in_dim(
        jnp.concatenate([pad, key_counts, pad]), place * blocks, window, 0
    )
    within = jnp.arange(BLK, dtype=jnp.int32)
    live = within[None, :] < counts[:, None]
    allowed = jnp.logical_and(block_mask[:, :, None] > 0, live[None])
    bias = jnp.where(allowed, 0.0, -1e30).astype(F32).reshape(blocks * 3, T)

    vmem = pl.BlockSpec(memory_space=pltpu.VMEM)
    buffers = [
        ((T, D), BF),
        ((ZH, Y, 2, ROWS, T), BF),
        ((ZH, Y, 2, ROWS, T), BF),
        ((ZH, Y, ROWS, T), BF),
        ((ZH, Y, ROWS, T), BF),
        ((ZH, Y, 2, ROWS, COLS), BF),
        ((2, T, HEAD), BF),
        ((3, 2, T, HEAD), BF),
        ((3, T, T), F32),
        ((3, T, T), BF),
        ((3, T, T), BF),
        ((T, HEAD), F32),
        ((T, HEAD), BF),
        ((T, NOWN * HEAD), BF),
        ((ZH * Y // NOWN, 2, ROWS, NOWN * HEAD), BF),
        ((T, D // NOWN), BF),
        ((2, 2, T, HEAD), BF),
        ((2, 2, T, HEAD), BF),
        ((2, T, HEAD), F32),
        ((2, T, COLS), BF),
        ((Y, ZH, ROWS, COLS), F32),
        ((2, H, ZH, ROWS, COLS), BF),
        ((2, H, ZH, ROWS, COLS), BF),
        ((ZH, ROWS, COLS), BF),
        ((ZH, ROWS, COLS), BF),
    ]
    sems = [
        (2, ZH), (2, 2, H, ZH), (2, Y), (2, 2, 2), (2, 2), (2, NOWN), (2, NOWN), (2, 2), (2, 2),
        (2, 2, H, ZH), (2, ZH), (2, NOWN), (3,),
    ]
    mixed, gq, go = pl.pallas_call(
        functools.partial(kernel, dims),
        out_shape=(
            jax.ShapeDtypeStruct((T, D), BF),
            jax.ShapeDtypeStruct((ROWS, 3 * HEAD), F32),
            jax.ShapeDtypeStruct((ROWS, HEAD), F32),
        ),
        in_specs=[vmem] * 5,
        out_specs=(vmem,) * 3,
        scratch_shapes=[pltpu.VMEM(s, t) for s, t in buffers]
        + [pltpu.SemaphoreType.DMA(s) for s in sems],
        compiler_params=pltpu.CompilerParams(
            collective_id=0, has_side_effects=True, vmem_limit_bytes=50 * 1024 * 1024
        ),
        cost_estimate=pl.CostEstimate(
            flops=2_600_000_000, bytes_accessed=6_000_000, transcendentals=500_000
        ),
    )(tokens, norm_gain.reshape(1, D), wblk, bias, upstream)
    return mixed, gq.reshape(ROWS, 3, HEAD), go


def build(torus):
    s = torus.shape
    dims = (s["zh"], s["y"], s["zl"], s["x"])
    placed = (
        P(DP, None), P(), P(DP, None, OWN), P(DP, None, OWN), P(DP, OWN), P(DP, OWN), P(DP, None),
        P(), P(DP, None),
    )
    return jax.shard_map(
        functools.partial(per_device, dims),
        mesh=torus,
        in_specs=placed,
        out_specs=(P(DP, None), P(DP, None, OWN), P(DP, OWN)),
        check_vma=False,
    )


def solution(mesh):
    return build(Mesh(mesh.devices.reshape(4, 8, 2, 2, 4), AXES))
```

time: 300 us -> 100 us (0.33); the launches traced: 296 us -> 99.8 us
  waiting for transfers between devices: 128 us -> 0 us
  Pallas kernels: 0 us -> 90.7 us
  starting transfers between devices: 85.8 us -> 0 us
  local copies, waits for them, and re-layouts: 36.6 us -> 5.24 us
  blocking collectives: 17.4 us -> 0 us
  other arithmetic: 16.7 us -> 3.18 us
  matrix products: 11 us -> 0 us
    all_to_all x10 -> x0, waiting for transfers between devices: 127 us -> none  [the longest x1 64.3 us: summed_rows(): lax.all_to_all(nearer, far, split_axis=0, concat_axis=0, tiled=True)]
    pallas_call x0 -> x1, Pallas kernels: none -> 90.7 us  [per_device(): pl.pallas_call(functools.partial(kernel, dims), out_shape=(jax.ShapeDtype...]
    all_to_all x10 -> x0, starting transfers between devices: 72.5 us -> none  [the longest x7 45.3 us: from_everyone(): return lax.all_to_all(copies, axis, split_axis=0, concat_axis=0, tiled=True)]
    all_to_all x3 -> x0, blocking collectives: 17.4 us -> none  [from_everyone(): return lax.all_to_all(copies, axis, split_axis=0, concat_axis=0, tiled=True)]
    ppermute x4 -> x0, starting transfers between devices: 13.3 us -> none  [the longest x2 6.29 us: from_behind(): return lax.ppermute(block, axis, route)]
    dot_general x11 -> x0, matrix products: 11 us -> none  [the longest x1 2.27 us: attend_backward(): jnp.einsum('qhe,khe->hqk', datt_h, value_h, preferred_element_type=jnp.fl...]
    reduce_sum x3 -> x0, other arithmetic: 7.76 us -> none  [the longest x1 4.23 us: sent_and_summed(): return jnp.sum(tiles, axis=0)]
    convert_element_type x10 -> x0, other arithmetic: 5.66 us -> none  [the longest x2 2.27 us: dequant_rows(): return (grouped * scales[..., None]).reshape(shape).astype(jnp.bfloat16)]
  transfers between devices with their start and end apart: 14 -> 0, of which waited for: 9 -> 0; matrix products, arithmetic and copies ran while one was open for 18% -> 0% of each run, Pallas kernels for 0% -> 0%
where the time goes in v1:
time: 100 us; the launch traced here: 99.8 us
  Pallas kernels  90.7 us (91%)
  local copies, waits for them, and re-layouts  5.24 us (5%)
  other arithmetic  3.18 us (3%)
    pallas_call x1, Pallas kernels, per_device(): pl.pallas_call(functools.partial(kernel, dims), out_shape=(jax.ShapeDtype...  90.7 us
    unnamed x8, local copies, waits for them, and re-layouts  5.15 us

profile of v1, /device:TPU:1, one launch (start us, length us, event | category | flops | bytes accessed | tf_op | source)
XLA Modules:
  0.0 99.8 jit_solution(5860125824544731961)
XLA Ops:
  0.6 0.7 broadcast_compare_fusion
  1.3 0.8 pad_add_fusion
  2.1 0.1 dynamic_slice.3
  2.2 0.1 iota_compare_fusion
  2.2 0.7 copy.22
  2.9 0.8 multiply_convert_fusion.1
  3.7 0.1 and_select_fusion
  3.8 0.8 copy_bitcast_fusion.1
  4.6 0.0 copy-start
  4.6 1.4 %copy-done = bf16[384,2048]{1,0:T(8,128)(2,1)S(1)} copy-done((bf16[384,2048]{1,0:T(8,128)(2,1)S(1)}, bf16[384,2048]{1,0:T(8,128)(2,1)}, u32[]{:S(2)}) %copy-start) | copy-done | bytes 1572888
  6.0 0.0 copy-start.1
  6.0 0.7 copy-done.1
  6.7 90.7 %shard_map.112 = (bf16[384,2048]{1,0:T(8,128)(2,1)S(1)}, f32[32,384]{1,0:T(8,128)S(1)}, f32[32,128]{1,0:T(8,128)S(1)}) custom-call(bf16[384,2048]{1,0:T(8,128)(2,1)S(1)} %copy-done, f32[1,2048]{1,0:T(1,128)S(1)} %bitcast.15, bf16[32,512]{1,0:T(8,128)(2,1)S(1)} %pad_maximum_fusion.wblk, f32[9,384]{1,0:T(8,128)S(1)} %select_n.13.bias, bf16[384,2048]{1,0:T(8,128)(2,1)} %ups.1), custom_call_target="tpu_custom_call" | custom-call | flops 2600000000 | bytes 6000000 | tf_op jit(solution)/shard_map/pallas_call | solution.py:407
  97.4 0.6 copy_bitcast_fusion
  98.0 1.1 %copy.25 = bf16[384,2048]{1,0:T(8,128)(2,1)} copy(bf16[384,2048]{1,0:T(8,128)(2,1)S(1)} %get-tuple-element.18) | data formatting | bytes 3145728
  99.2 0.6 copy.26
  (3 shorter events, 0.0 us)
Async XLA Ops:
  4.6 1.4 %copy-start = (bf16[384,2048]{1,0:T(8,128)(2,1)S(1)}, bf16[384,2048]{1,0:T(8,128)(2,1)}, u32[]{:S(2)}) copy-start(bf16[384,2048]{1,0:T(8,128)(2,1)} %tok.1) | copy-start | bytes 4718596
  6.0 0.7 copy-start.1

commit v2 on v1

v2 whole, which is shorter than its diff:
```python
import functools
import math

import jax
import jax.numpy as jnp
from jax import lax
from jax.experimental import pallas as pl
from jax.experimental.pallas import tpu as pltpu
from jax.sharding import Mesh
from jax.sharding import PartitionSpec as P

HEAD = 128
BLK = 128
ROWS = 32
COLS = 4 * HEAD
AXES = ("zh", "y", "core", "zl", "x")
DP = ("zh", "y", "core")
OWN = ("zl", "x")
BF = jnp.bfloat16
F32 = jnp.float32
MESH = pl.DeviceIdType.MESH
INV_ROOT = 1.0 / HEAD**0.5
TO_EXP2 = INV_ROOT * math.log2(math.e)


def nn(a, b):
    return lax.dot_general(a, b, (((1,), (0,)), ((), ())), preferred_element_type=F32)


def nt(a, b):
    return lax.dot_general(a, b, (((1,), (1,)), ((), ())), preferred_element_type=F32)


def tn(a, b):
    return lax.dot_general(a, b, (((0,), (0,)), ((), ())), preferred_element_type=F32)


def kernel(
    dims,
    tok_hbm, gain, codes, scales, ocodes, oscales, maskb, counts, ups_hbm,
    mixed, gq, go,
    tok, ups, bias, normed, ntr, utr, nts, uts, wbuf, wof, qd, kv, ebuf, pbuf, dsb, dqa, atts,
    att_all, hgs, hgr, ogr, dd, g, rss, rsr, fin, zs, zr,
    agz, agy, ags, halo, tsw, wos, wps, ats, hgm, dds, rsm, zsm, loc,
):
    ZH, Y, ZL, X = dims
    H = Y // 2
    ZP = ZH // 2
    W = 2 * HEAD
    NOWN = ZL * X
    T, D = tok.shape
    NQ = T // BLK
    SEG = T // BLK
    zh, y, c = lax.axis_index("zh"), lax.axis_index("y"), lax.axis_index("core")
    own = lax.axis_index("zl") * X + lax.axis_index("x")
    sib = {"core": 1 - c}
    pending = {}
    locals_ = []

    def rcopy(src, dst, sems, index, dev):
        return pltpu.make_async_remote_copy(
            src_ref=src,
            dst_ref=dst,
            send_sem=sems.at[(0, *index)],
            recv_sem=sems.at[(1, *index)],
            device_id=dev,
            device_id_type=MESH,
        )

    def send(src, dst, sems, index, dev):
        cp = rcopy(src, dst, sems, index, dev)
        cp.start()
        pending[id(sems), index] = [cp, True]

    def arrived(dst, sems, index):
        rcopy(dst, dst, sems, index, sib).wait_recv()
        pending[id(sems), index][1] = False

    def finish():
        for cp in locals_:
            cp.wait()
        for cp, due in pending.values():
            if due:
                cp.wait_recv()
            cp.wait_send()

    def keep(src, dst, i):
        cp = pltpu.make_async_copy(src, dst, loc.at[i])
        cp.start()
        return cp

    def zk(k):
        return lax.rem(zh + k, ZH)

    def yd(d):
        return lax.rem(y + (d + Y), Y)

    def ydev(d):
        return {"y": yd(d)}

    def owner(j):
        return lax.rem(own + j, NOWN)

    def odev(o):
        return {"zl": o // X, "x": lax.rem(o, X)}

    def lanes(o, n):
        return pl.ds(pl.multiple_of(o * n, n), n)

    place = (zh * Y + y) * 2 + c
    count = ZH * Y * 2

    def range_dev(step):
        r = lax.rem(place + step + count, count)
        return {"zh": r // (2 * Y), "y": lax.rem(r // 2, Y), "core": lax.rem(r, 2)}

    nxt, prv = range_dev(1), range_dev(-1)

    barrier = pltpu.get_barrier_semaphore()
    partners = [odev(owner(j)) for j in range(1, NOWN)]
    partners += [{"zh": zk(k)} for k in range(1, ZH)]
    partners += [nxt, prv, ydev(1), ydev(-1), sib]
    for dev in partners:
        pl.semaphore_signal(barrier, inc=1, device_id=dev, device_id_type=MESH)
    load_tok = keep(tok_hbm, tok, 0)
    load_ups = keep(ups_hbm, ups, 1)

    eye = lax.broadcasted_iota(jnp.int32, (ROWS, ROWS), 0) == lax.broadcasted_iota(
        jnp.int32, (ROWS, ROWS), 1
    )

    def column(row):
        return jnp.sum(jnp.where(eye, row, 0.0), axis=1, keepdims=True)

    for at, j in enumerate((1, 2, 0)):
        part = codes[j].astype(F32) * column(scales[j])
        wbuf[zh, y, c, :, at * HEAD : (at + 1) * HEAD] = part.astype(BF)
    part = ocodes[...].astype(F32) * column(oscales[...])
    wbuf[zh, y, c, :, 3 * HEAD :] = part.astype(BF)

    blocks = lax.broadcasted_iota(jnp.int32, counts.shape, 1)
    within = lax.broadcasted_iota(jnp.int32, (1, BLK), 1)
    for j in range(3 * SEG):
        which = place * SEG + (j - SEG)
        alive = jnp.sum(jnp.where(blocks == which, counts[...], 0), axis=1, keepdims=True)
        for b in range(NQ):
            ok = jnp.logical_and(within < alive, maskb[b : b + 1, j : j + 1] > 0)
            row = b * 3 + j // SEG
            lo = (j % SEG) * BLK
            bias[row : row + 1, lo : lo + BLK] = jnp.where(ok, 0.0, -1e30)
    pl.semaphore_wait(barrier, len(partners))

    def cols(h):
        return pl.ds(h * W, W)

    def piece(h, q, d):
        return wbuf.at[pl.ds(q * ZP, ZP), yd(d), c, :, cols(h)]

    def ag_send(d, t, h, q):
        s = 1 if d == 0 else -1
        b = piece(h, q, -s * (t - 1))
        send(b, b, agy, (d, t - 1, h, q), ydev(s))

    def ag_wait(d, t, h, q):
        s = 1 if d == 0 else -1
        arrived(piece(h, q, -s * t), agy, (d, t - 1, h, q))

    def ag_pass(h, dy):
        b = wbuf.at[:, yd(dy), c, :, cols(h)]
        send(b, b, ags, (h, dy % Y), sib)

    def wof_send(dy):
        src = wbuf.at[:, yd(dy), c, :, pl.ds(3 * HEAD, HEAD)]
        for j in range(1, NOWN):
            o = owner(j)
            rcopy(src, wof.at[:, yd(dy), c, :, lanes(own, HEAD)], wos, (j,), odev(o)).start()

    def ag_z(h):
        for k in range(1, ZH):
            arrived(wbuf.at[zk(ZH - k), y, c, :, cols(h)], agz, (h, k))
        for q in range(2):
            for d in range(2):
                ag_send(d, 1, h, q)
        ag_pass(h, 0)

    for h in range(2):
        mine = wbuf.at[zh, y, c, :, cols(h)]
        for k in (2, 1, 3)[: ZH - 1] if ZH == 4 else range(1, ZH):
            send(mine, mine, agz, (h, k), {"zh": zk(k)})

    def norm_rows(i, carry):
        r = pl.ds(pl.multiple_of(i * 16, 16), 16)
        x = tok[r, :].astype(F32)
        factor = lax.rsqrt(jnp.mean(x * x, axis=-1, keepdims=True) + 1e-05)
        normed[r, :] = (x * factor * gain[...]).astype(BF)
        return carry

    def turn(src, dst):
        per = Y // 2

        def body(j, carry):
            v = src[:, pl.ds(pl.multiple_of(j * 128, 128), 128)]
            dst[j // per, pl.ds(2 * lax.rem(j, per), 2)] = v.T.reshape(2, 2, ROWS, T)
            return carry

        return body

    load_tok.wait()
    lax.fori_loop(0, T // 16, norm_rows, 0)
    ag_z(0)
    ag_z(1)
    wof_send(0)
    load_ups.wait()

    def fill(t):
        if t == 1:
            lax.fori_loop(0, D // 128, turn(ups, utr), 0)
            send(utr.at[:, :, 1 - c], uts, tsw, (0,), sib)
        if t == 2:
            lax.fori_loop(0, D // 128, turn(normed, ntr), 0)
            send(ntr.at[:, :, 1 - c], nts, tsw, (1,), sib)

    for t in range(1, H + 1):
        for h in range(2):
            for q in range(2):
                for d in range(2):
                    if t == H and q != d:
                        continue
                    ag_wait(d, t, h, q)
                    if t < H - 1 or (t == H - 1 and q == d):
                        ag_send(d, t + 1, h, q)
            ag_pass(h, -t)
            if t < H:
                ag_pass(h, t)
        wof_send(-t)
        if t < H:
            wof_send(t)
        fill(t)

    def from_sibling(h):
        for dy in range(Y):
            arrived(wbuf.at[:, yd(dy), 1 - c, :, cols(h)], ags, (h, dy))

    def project(src, lo, n):
        total = None
        for z in range(ZH):
            w = wbuf[z, :, :, :, lo : lo + n].reshape(Y * 2 * ROWS, n)
            term = nn(src[:, z * Y * 64 : (z + 1) * Y * 64], w)
            total = term if total is None else total + term
        return total.astype(BF)

    from_sibling(0)
    keyval = project(normed, 0, W)
    kv[1, 0] = keyval[:, :HEAD]
    kv[1, 1] = keyval[:, HEAD:]
    for j in range(2):
        send(kv.at[1, j], kv.at[0, j], halo, (0, j), nxt)
        send(kv.at[1, j], kv.at[2, j], halo, (1, j), prv)
    from_sibling(1)
    qd[0] = project(normed, W, HEAD)
    qd[1] = project(ups, 3 * HEAD, HEAD)
    keep_wo = keep(
        wbuf.at[:, :, :, :, pl.ds(3 * HEAD, HEAD)], wof.at[:, :, :, :, lanes(own, HEAD)], 2
    )

    sums = [None] * NQ
    for seg in (1, 0, 2):
        if seg != 1:
            arrived(kv.at[seg, 0], halo, (seg // 2, 0))
        for b in range(NQ):
            rows = slice(b * BLK, (b + 1) * BLK)
            score = nt(qd[0, rows, :], kv[seg, 0])
            e = jnp.exp2(score * TO_EXP2 + bias[b * 3 + seg : b * 3 + seg + 1, :])
            ebuf[seg, rows, :] = e
            part = jnp.sum(e, axis=-1, keepdims=True)
            sums[b] = part if sums[b] is None else sums[b] + part
    for seg in (0, 2):
        arrived(kv.at[seg, 1], halo, (seg // 2, 1))
    deltas = []
    for b in range(NQ):
        rows = slice(b * BLK, (b + 1) * BLK)
        scale = 1.0 / sums[b]
        total = None
        for seg in range(3):
            p = ebuf[seg, rows, :] * scale
            ebuf[seg, rows, :] = p
            pb = p.astype(BF)
            pbuf[seg, rows, :] = pb
            term = nn(pb, kv[seg, 1])
            total = term if total is None else total + term
        atts[rows, :] = total.astype(BF)
        deltas.append(jnp.sum(total * qd[1, rows, :].astype(F32), axis=-1, keepdims=True))
    dd[0, :, 3 * HEAD :] = atts[...]
    send(dd.at[0, :, pl.ds(3 * HEAD, HEAD)], dd.at[1, :, pl.ds(3 * HEAD, HEAD)], dds, (0,), sib)
    for j in range(1, NOWN):
        send(atts, att_all.at[:, lanes(own, HEAD)], ats, (j,), odev(owner(j)))
    keep_att = keep(atts, att_all.at[:, lanes(own, HEAD)], 3)

    for seg in (0, 2, 1):
        for b in range(NQ):
            rows = slice(b * BLK, (b + 1) * BLK)
            dp = nt(qd[1, rows, :], kv[seg, 1])
            ds = (ebuf[seg, rows, :] * (dp - deltas[b]) * INV_ROOT).astype(BF)
            dsb[seg, rows, :] = ds
            term = nn(ds, kv[seg, 0])
            if seg == 0:
                dqa[rows, :] = term
            else:
                dqa[rows, :] += term
        if seg == 1:
            dd[0, :, W : 3 * HEAD] = dqa[...].astype(BF)
            part = pl.ds(W, HEAD)
            send(dd.at[0, :, part], dd.at[1, :, part], dds, (1,), sib)
        dk = tn(dsb[seg], qd[0])
        dv = tn(pbuf[seg], qd[1])
        if seg == 1:
            ogr[0] = dk
            ogr[1] = dv
        else:
            hgs[seg // 2, 0] = dk.astype(BF)
            hgs[seg // 2, 1] = dv.astype(BF)
            send(hgs.at[seg // 2], hgr.at[seg // 2], hgm, (seg // 2,), prv if seg == 0 else nxt)

    high = ZH * ROWS

    def pair(own_rows, sib_rows, dy, lo, n):
        yy = yd(dy)
        a = nn(own_rows[:, yy, c].reshape(high, T), dd[0, :, lo : lo + n])
        a += nn(sib_rows[:, yy].reshape(high, T), dd[1, :, lo : lo + n])
        return a.reshape(ZH, ROWS, n)

    def term_at(h, dy):
        if h == 0:
            g[0, dy % Y] = pair(ntr, nts, dy, 0, W)
        else:
            g[1, dy % Y, :, :, :HEAD] = pair(ntr, nts, dy, W, HEAD)
            g[1, dy % Y, :, :, HEAD:] = pair(utr, uts, dy, W + HEAD, HEAD)

    def zrange(q):
        return pl.ds(q * ZP, ZP)

    def rs_terms(h, t):
        term_at(h, H - t)
        if t > 0:
            term_at(h, t - H)
        if t == H - 1:
            term_at(h, 0)

    def rs_step(h, t):
        for q in range(2):
            for d in range(2):
                s = 1 if d == 0 else -1
                if t == 0 and q != d:
                    continue
                val = g[h, (s * (H - t)) % Y, zrange(q)]
                if t > 1 or (t == 1 and q == d):
                    arrived(rsr.at[h, d, t - 1, q], rsm, (h, d, t - 1, q))
                    val += rsr[h, d, t - 1, q].astype(F32)
                rss[h, d, t, q] = val.astype(BF)
                send(rss.at[h, d, t, q], rsr.at[h, d, t, q], rsm, (h, d, t, q), ydev(s))

    def rs_last(h):
        for q in range(2):
            val = g[h, 0, zrange(q)]
            for d in range(2):
                arrived(rsr.at[h, d, H - 1, q], rsm, (h, d, H - 1, q))
                val += rsr[h, d, H - 1, q].astype(F32)
            fin[h, zrange(q)] = val
        for k in (2, 1, 3)[: ZH - 1] if ZH == 4 else range(1, ZH):
            zs[h, k] = fin[h, zk(k)].astype(BF)
            send(zs.at[h, k], zr.at[h, k], zsm, (h, k), {"zh": zk(k)})

    def rs_end(h):
        val = fin[h, zh]
        for k in range(1, ZH):
            arrived(zr.at[h, k], zsm, (h, k))
            val += zr[h, k].astype(F32)
        return val

    def wof_part(o, core):
        return wof.at[:, :, core, :, lanes(o, HEAD)]

    def wof_pass():
        for j in range(1, NOWN):
            part = wof_part(owner(NOWN - j), c)
            rcopy(part, part, wos, (j,), sib).wait_recv()
            send(part, part, wps, (j,), sib)

    def mix_wait():
        keep_wo.wait()
        keep_att.wait()
        for j in range(1, NOWN):
            o = owner(NOWN - j)
            arrived(wof_part(o, 1 - c), wps, (j,))
            arrived(att_all.at[:, lanes(o, HEAD)], ats, (j,))

    def mix(z):
        n = D // ZH
        w = wof[z].reshape(n, NOWN * HEAD)
        for b in range(NQ):
            rows = slice(b * BLK, (b + 1) * BLK)
            mixed[rows, z * n : (z + 1) * n] = nt(att_all[rows, :], w).astype(BF)

    arrived(uts, tsw, (0,))
    arrived(nts, tsw, (1,))
    arrived(dd.at[1, :, pl.ds(3 * HEAD, HEAD)], dds, (0,))
    arrived(dd.at[1, :, pl.ds(W, HEAD)], dds, (1,))
    rs_terms(1, 0)
    rs_step(1, 0)
    rs_terms(1, 1)
    for side in range(2):
        arrived(hgr.at[side], hgm, (side,))
    for j in range(2):
        both = ogr[j] + hgr[0, j].astype(F32) + hgr[1, j].astype(F32)
        dd[0, :, j * HEAD : (j + 1) * HEAD] = both.astype(BF)
    send(dd.at[0, :, pl.ds(0, W)], dd.at[1, :, pl.ds(0, W)], dds, (2,), sib)
    rs_step(1, 1)
    rs_terms(1, 2)
    arrived(dd.at[1, :, pl.ds(0, W)], dds, (2,))
    rs_terms(0, 0)
    rs_step(0, 0)
    rs_terms(0, 1)
    for t in range(2, H):
        rs_step(1, t)
        rs_terms(1, t + 1) if t + 1 < H else None
        rs_step(0, t - 1)
        rs_terms(0, t)
        if t == 2:
            wof_pass()
    rs_last(1)
    rs_step(0, H - 1)
    mix_wait()
    for z in range(ZH // 2):
        mix(z)
    rs_last(0)
    for z in range(ZH // 2, ZH):
        mix(z)
    early = rs_end(1)
    gq[0] = early[:, :HEAD]
    go[...] = early[:, HEAD:]
    late = rs_end(0)
    gq[1] = late[:, :HEAD]
    gq[2] = late[:, HEAD:]
    part = wbuf.at[:, :, c, :, pl.ds(3 * HEAD, HEAD)]
    for j in range(1, NOWN):
        rcopy(part, wof_part(own, c), wos, (j,), odev(owner(j))).wait_send()
    finish()


def per_device(
    dims,
    tokens, norm_gain, qkv_codes, qkv_scales, out_codes, out_scales, block_mask, key_counts, upstream,
):
    ZH, Y, ZL, X = dims
    H = Y // 2
    NOWN = ZL * X
    T, D = tokens.shape
    W = 2 * HEAD
    vmem = pl.BlockSpec(memory_space=pltpu.VMEM)
    far = pl.BlockSpec(memory_space=pltpu.HBM)
    buffers = [
        ((T, D), BF),
        ((T, D), BF),
        ((9, T), F32),
        ((T, D), BF),
        ((ZH, Y, 2, ROWS, T), BF),
        ((ZH, Y, 2, ROWS, T), BF),
        ((ZH, Y, ROWS, T), BF),
        ((ZH, Y, ROWS, T), BF),
        ((ZH, Y, 2, ROWS, COLS), BF),
        ((ZH, Y, 2, ROWS, NOWN * HEAD), BF),
        ((2, T, HEAD), BF),
        ((3, 2, T, HEAD), BF),
        ((3, T, T), F32),
        ((3, T, T), BF),
        ((3, T, T), BF),
        ((T, HEAD), F32),
        ((T, HEAD), BF),
        ((T, NOWN * HEAD), BF),
        ((2, 2, T, HEAD), BF),
        ((2, 2, T, HEAD), BF),
        ((2, T, HEAD), F32),
        ((2, T, COLS), BF),
        ((2, Y, ZH, ROWS, W), F32),
        ((2, 2, H, 2, ZH // 2, ROWS, W), BF),
        ((2, 2, H, 2, ZH // 2, ROWS, W), BF),
        ((2, ZH, ROWS, W), F32),
        ((2, ZH, ROWS, W), BF),
        ((2, ZH, ROWS, W), BF),
    ]
    sems = [
        (2, 2, ZH), (2, 2, H, 2, 2), (2, 2, Y), (2, 2, 2), (2, 2), (2, NOWN), (2, NOWN), (2, NOWN),
        (2, 2), (2, 3), (2, 2, 2, H, 2), (2, 2, ZH), (4,),
    ]
    mixed, gq, go = pl.pallas_call(
        functools.partial(kernel, dims),
        out_shape=(
            jax.ShapeDtypeStruct((T, D), BF),
            jax.ShapeDtypeStruct((3, ROWS, HEAD), F32),
            jax.ShapeDtypeStruct((ROWS, HEAD), F32),
        ),
        in_specs=[far] + [vmem] * 7 + [far],
        out_specs=(vmem,) * 3,
        scratch_shapes=[pltpu.VMEM(s, t) for s, t in buffers]
        + [pltpu.SemaphoreType.DMA(s) for s in sems],
        compiler_params=pltpu.CompilerParams(
            collective_id=0, has_side_effects=True, vmem_limit_bytes=63 * 1024 * 1024
        ),
        cost_estimate=pl.CostEstimate(
            flops=4_000_000_000, bytes_accessed=6_000_000, transcendentals=500_000
        ),
    )(
        tokens,
        norm_gain.reshape(1, D),
        qkv_codes.transpose(1, 0, 2),
        qkv_scales.transpose(1, 2, 0),
        out_codes,
        out_scales.transpose(1, 0),
        block_mask,
        key_counts.reshape(1, -1),
        upstream,
    )
    return mixed, gq.transpose(1, 0, 2), go


def build(torus):
    s = torus.shape
    dims = (s["zh"], s["y"], s["zl"], s["x"])
    placed = (
        P(DP, None), P(), P(DP, None, OWN), P(DP, None, OWN), P(DP, OWN), P(DP, OWN), P(DP, None),
        P(), P(DP, None),
    )
    return jax.shard_map(
        functools.partial(per_device, dims),
        mesh=torus,
        in_specs=placed,
        out_specs=(P(DP, None), P(DP, None, OWN), P(DP, OWN)),
        check_vma=False,
    )


def solution(mesh):
    return build(Mesh(mesh.devices.reshape(4, 8, 2, 2, 4), AXES))
```

time: 100 us -> 81.9 us (0.82); the launches traced: 99.8 us -> 80.5 us
  Pallas kernels: 90.7 us -> 75.8 us
  other arithmetic: 3.18 us -> 0 us
  local copies, waits for them, and re-layouts: 5.24 us -> 3.98 us
    pallas_call x1, Pallas kernels: 90.7 us -> 75.8 us  [per_device(): pl.pallas_call(functools.partial(kernel, dims), out_shape=(jax.ShapeDtype...]
    unnamed x8 -> x7, local copies, waits for them, and re-layouts: 5.15 us -> 3.98 us
where the time goes in v2:
time: 81.9 us; the launch traced here: 80.5 us
  Pallas kernels  75.8 us (93%)
  local copies, waits for them, and re-layouts  3.98 us (5%)
    pallas_call x1, Pallas kernels, per_device(): pl.pallas_call(functools.partial(kernel, dims), out_shape=(jax.ShapeDtype...  75.8 us
    unnamed x7, local copies, waits for them, and re-layouts  3.98 us

profile of v2, /device:TPU:1, one launch (start us, length us, event | category | flops | bytes accessed | tf_op | source)
XLA Modules:
  0.0 80.5 jit_solution(4355259956614772155)
XLA Ops:
  0.6 75.8 %shard_map.112 = (bf16[384,2048]{1,0:T(8,128)(2,1)}, f32[3,32,128]{2,1,0:T(8,128)}, f32[32,128]{1,0:T(8,128)}) custom-call(bf16[384,2048]{1,0:T(8,128)(2,1)} %tok_hbm.1, f32[1,2048]{1,0:T(1,128)} %bitcast.8, bf16[3,32,128]{2,1,0:T(8,128)(2,1)} %bitcast.7, f32[3,1,32]{2,1,0:T(1,128)} %bitcast.9, bf16[32,128]{1,0:T(8,128)(2,1)} %ocodes.1, f32[1,32]{1,0:T(1,128)} %bitcast.11, ...), custom_call_target="tpu_custom_call" | custom-call | flops 4000000000 | bytes 6000000 | tf_op jit(solution)/shard_map/pallas_call | solution.py:495
  76.5 0.0 copy-start
  76.5 0.0 copy-start.1
  76.5 2.7 %copy.15 = bf16[384,2048]{1,0:T(8,128)(2,1)} copy(bf16[384,2048]{1,0:T(8,128)(2,1)} %get-tuple-element.12) | data formatting | bytes 3145728
  79.3 0.0 copy-done
  79.3 0.6 copy.16
  79.9 0.0 copy-done.1
  79.9 0.6 copy.17
Async XLA Ops:
  76.5 2.8 %copy-start = (f32[3,32,128]{2,1,0:T(8,128)S(1)}, f32[3,32,128]{2,1,0:T(8,128)}, u32[]{:S(2)}) copy-start(f32[3,32,128]{2,1,0:T(8,128)} %get-tuple-element.7) | copy-start | bytes 147460
  76.5 3.4 %copy-start.1 = (f32[32,128]{1,0:T(8,128)S(1)}, f32[32,128]{1,0:T(8,128)}, u32[]{:S(2)}) copy-start(f32[32,128]{1,0:T(8,128)} %get-tuple-element.14) | copy-start | bytes 49156

commit v3 on v2

--- a/solution.py
+++ b/solution.py
@@ -119,7 +119,7 @@
     barrier = pltpu.get_barrier_semaphore()
     partners = [odev(owner(j)) for j in range(1, NOWN)]
     partners += [{"zh": zk(k)} for k in range(1, ZH)]
-    partners += [nxt, prv, ydev(1), ydev(-1), sib]
+    partners += [nxt, prv, ydev(2), ydev(-2), ydev(1), ydev(-1), sib]
     for dev in partners:
         pl.semaphore_signal(barrier, inc=1, device_id=dev, device_id_type=MESH)
     load_tok = keep(tok_hbm, tok, 0)
@@ -134,9 +134,10 @@
 
     for at, j in enumerate((1, 2, 0)):
         part = codes[j].astype(F32) * column(scales[j])
-        wbuf[zh, y, c, :, at * HEAD : (at + 1) * HEAD] = part.astype(BF)
+        lo = (at % 2) * HEAD
+        wbuf[at // 2, zh, y, c, :, lo : lo + HEAD] = part.astype(BF)
     part = ocodes[...].astype(F32) * column(oscales[...])
-    wbuf[zh, y, c, :, 3 * HEAD :] = part.astype(BF)
+    wbuf[1, zh, y, c, :, HEAD:] = part.astype(BF)
 
     blocks = lax.broadcasted_iota(jnp.int32, counts.shape, 1)
     within = lax.broadcasted_iota(jnp.int32, (1, BLK), 1)
@@ -150,41 +151,43 @@
             bias[row : row + 1, lo : lo + BLK] = jnp.where(ok, 0.0, -1e30)
     pl.semaphore_wait(barrier, len(partners))
 
-    def cols(h):
-        return pl.ds(h * W, W)
-
     def piece(h, q, d):
-        return wbuf.at[pl.ds(q * ZP, ZP), yd(d), c, :, cols(h)]
+        return wbuf.at[h, pl.ds(q * ZP, ZP), yd(d), c]
 
     def ag_send(d, t, h, q):
         s = 1 if d == 0 else -1
         b = piece(h, q, -s * (t - 1))
         send(b, b, agy, (d, t - 1, h, q), ydev(s))
 
+    def ag_skip(d, h, q):
+        s = 1 if d == 0 else -1
+        b = piece(h, q, -s * (H - 2))
+        send(b, b, agy, (d, H - 1, h, q), ydev(2 * s))
+
     def ag_wait(d, t, h, q):
         s = 1 if d == 0 else -1
         arrived(piece(h, q, -s * t), agy, (d, t - 1, h, q))
 
     def ag_pass(h, dy):
-        b = wbuf.at[:, yd(dy), c, :, cols(h)]
+        b = wbuf.at[h, :, yd(dy), c]
         send(b, b, ags, (h, dy % Y), sib)
 
     def wof_send(dy):
-        src = wbuf.at[:, yd(dy), c, :, pl.ds(3 * HEAD, HEAD)]
+        src = wbuf.at[1, :, yd(dy), c, :, pl.ds(HEAD, HEAD)]
         for j in range(1, NOWN):
             o = owner(j)
             rcopy(src, wof.at[:, yd(dy), c, :, lanes(own, HEAD)], wos, (j,), odev(o)).start()
 
     def ag_z(h):
         for k in range(1, ZH):
-            arrived(wbuf.at[zk(ZH - k), y, c, :, cols(h)], agz, (h, k))
+            arrived(wbuf.at[h, zk(ZH - k), y, c], agz, (h, k))
         for q in range(2):
             for d in range(2):
                 ag_send(d, 1, h, q)
         ag_pass(h, 0)
 
     for h in range(2):
-        mine = wbuf.at[zh, y, c, :, cols(h)]
+        mine = wbuf.at[h, zh, y, c]
         for k in (2, 1, 3)[: ZH - 1] if ZH == 4 else range(1, ZH):
             send(mine, mine, agz, (h, k), {"zh": zk(k)})
 
@@ -220,47 +223,51 @@
             lax.fori_loop(0, D // 128, turn(normed, ntr), 0)
             send(ntr.at[:, :, 1 - c], nts, tsw, (1,), sib)
 
-    for t in range(1, H + 1):
+    for t in range(1, H):
         for h in range(2):
             for q in range(2):
                 for d in range(2):
-                    if t == H and q != d:
-                        continue
                     ag_wait(d, t, h, q)
-                    if t < H - 1 or (t == H - 1 and q == d):
+                    if t < H - 1:
                         ag_send(d, t + 1, h, q)
+                    if t == H - 2 and q == d:
+                        ag_skip(d, h, q)
             ag_pass(h, -t)
-            if t < H:
-                ag_pass(h, t)
+            ag_pass(h, t)
+            if t == H - 1:
+                for d in range(2):
+                    ag_wait(d, H, h, d)
+                ag_pass(h, H)
         wof_send(-t)
-        if t < H:
-            wof_send(t)
+        wof_send(t)
+        if t == H - 1:
+            wof_send(H)
         fill(t)
 
     def from_sibling(h):
         for dy in range(Y):
-            arrived(wbuf.at[:, yd(dy), 1 - c, :, cols(h)], ags, (h, dy))
-
-    def project(src, lo, n):
+            arrived(wbuf.at[h, :, yd(dy), 1 - c], ags, (h, dy))
+
+    def project(src, h, lo, n):
         total = None
         for z in range(ZH):
-            w = wbuf[z, :, :, :, lo : lo + n].reshape(Y * 2 * ROWS, n)
+            w = wbuf[h, z, :, :, :, lo : lo + n].reshape(Y * 2 * ROWS, n)
             term = nn(src[:, z * Y * 64 : (z + 1) * Y * 64], w)
             total = term if total is None else total + term
         return total.astype(BF)
 
     from_sibling(0)
-    keyval = project(normed, 0, W)
+    keyval = project(normed, 0, 0, W)
     kv[1, 0] = keyval[:, :HEAD]
     kv[1, 1] = keyval[:, HEAD:]
     for j in range(2):
         send(kv.at[1, j], kv.at[0, j], halo, (0, j), nxt)
         send(kv.at[1, j], kv.at[2, j], halo, (1, j), prv)
     from_sibling(1)
-    qd[0] = project(normed, W, HEAD)
-    qd[1] = project(ups, 3 * HEAD, HEAD)
+    qd[0] = project(normed, 1, 0, HEAD)
+    qd[1] = project(ups, 1, HEAD, HEAD)
     keep_wo = keep(
-        wbuf.at[:, :, :, :, pl.ds(3 * HEAD, HEAD)], wof.at[:, :, :, :, lanes(own, HEAD)], 2
+        wbuf.at[1, :, :, :, :, pl.ds(HEAD, HEAD)], wof.at[:, :, :, :, lanes(own, HEAD)], 2
     )
 
     sums = [None] * NQ
@@ -340,24 +347,31 @@
         return pl.ds(q * ZP, ZP)
 
     def rs_terms(h, t):
-        term_at(h, H - t)
-        if t > 0:
-            term_at(h, t - H)
-        if t == H - 1:
-            term_at(h, 0)
+        for dy in {0: (H, H - 1, 1 - H), 1: (H - 2, 2 - H), 2: (1, -1, 0)}[t]:
+            term_at(h, dy)
+
+    def rs_send(val, h, d, t, q, hops):
+        rss[h, d, t, q] = val.astype(BF)
+        send(rss.at[h, d, t, q], rsr.at[h, d, t, q], rsm, (h, d, t, q), ydev(hops))
+
+    def rs_got(h, d, t, q):
+        arrived(rsr.at[h, d, t, q], rsm, (h, d, t, q))
+        return rsr[h, d, t, q].astype(F32)
 
     def rs_step(h, t):
         for q in range(2):
             for d in range(2):
                 s = 1 if d == 0 else -1
-                if t == 0 and q != d:
-                    continue
-                val = g[h, (s * (H - t)) % Y, zrange(q)]
-                if t > 1 or (t == 1 and q == d):
-                    arrived(rsr.at[h, d, t - 1, q], rsm, (h, d, t - 1, q))
-                    val += rsr[h, d, t - 1, q].astype(F32)
-                rss[h, d, t, q] = val.astype(BF)
-                send(rss.at[h, d, t, q], rsr.at[h, d, t, q], rsm, (h, d, t, q), ydev(s))
+                far = H - 1 - t
+                val = g[h, (s * far) % Y, zrange(q)]
+                if t == 0:
+                    if q == d:
+                        rs_send(g[h, H, zrange(q)], h, d, 0, q, 2 * s)
+                else:
+                    val += rs_got(h, d, t, q)
+                    if t == 1 and q == d:
+                        val += rs_got(h, d, 0, q)
+                rs_send(val, h, d, t + 1, q, s)
 
     def rs_last(h):
         for q in range(2):
@@ -420,15 +434,12 @@
     rs_terms(0, 0)
     rs_step(0, 0)
     rs_terms(0, 1)
-    for t in range(2, H):
-        rs_step(1, t)
-        rs_terms(1, t + 1) if t + 1 < H else None
-        rs_step(0, t - 1)
-        rs_terms(0, t)
-        if t == 2:
-            wof_pass()
+    rs_step(1, 2)
+    rs_terms(0, 2)
+    rs_step(0, 1)
+    wof_pass()
     rs_last(1)
-    rs_step(0, H - 1)
+    rs_step(0, 2)
     mix_wait()
     for z in range(ZH // 2):
         mix(z)
@@ -441,10 +452,30 @@
     late = rs_end(0)
     gq[1] = late[:, :HEAD]
     gq[2] = late[:, HEAD:]
-    part = wbuf.at[:, :, c, :, pl.ds(3 * HEAD, HEAD)]
+    part = wbuf.at[1, :, :, c, :, pl.ds(HEAD, HEAD)]
     for j in range(1, NOWN):
         rcopy(part, wof_part(own, c), wos, (j,), odev(owner(j))).wait_send()
     finish()
+
+
+def store(*refs):
+    sources, results, held, sems = refs[:3], refs[3:6], refs[6:9], refs[9]
+    rows = sources[0].shape[0] // 4
+    parts = [(0, pl.ds(i * rows, rows)) for i in range(4)] + [(1, slice(None)), (2, slice(None))]
+    inward, outward = [], []
+    for i, (a, part) in enumerate(parts):
+        inward.append(
+            pltpu.make_async_copy(sources[a].at[part], held[a].at[part], sems.at[0, i])
+        )
+        outward.append(
+            pltpu.make_async_copy(held[a].at[part], results[a].at[part], sems.at[1, i])
+        )
+        inward[-1].start()
+    for first, second in zip(inward, outward):
+        first.wait()
+        second.start()
+    for second in outward:
+        second.wait()
 
 
 def per_device(
@@ -467,7 +498,7 @@
         ((ZH, Y, 2, ROWS, T), BF),
         ((ZH, Y, ROWS, T), BF),
         ((ZH, Y, ROWS, T), BF),
-        ((ZH, Y, 2, ROWS, COLS), BF),
+        ((2, ZH, Y, 2, ROWS, W), BF),
         ((ZH, Y, 2, ROWS, NOWN * HEAD), BF),
         ((2, T, HEAD), BF),
         ((3, 2, T, HEAD), BF),
@@ -520,6 +551,15 @@
         key_counts.reshape(1, -1),
         upstream,
     )
+    mixed, gq, go = pl.pallas_call(
+        store,
+        out_shape=tuple(jax.ShapeDtypeStruct(a.shape, a.dtype) for a in (mixed, gq, go)),
+        in_specs=[far] * 3,
+        out_specs=(far,) * 3,
+        scratch_shapes=[pltpu.VMEM(a.shape, a.dtype) for a in (mixed, gq, go)]
+        + [pltpu.SemaphoreType.DMA((2, 6))],
+        compiler_params=pltpu.CompilerParams(vmem_limit_bytes=63 * 1024 * 1024),
+    )(mixed, gq, go)
     return mixed, gq.transpose(1, 0, 2), go
 
 

time: 81.9 us -> 76.2 us (0.930); the launches traced: 80.5 us -> 76 us
  local copies, waits for them, and re-layouts: 3.98 us -> 0 us
    unnamed x7 -> x0, local copies, waits for them, and re-layouts: 3.98 us -> none
    pallas_call x1, Pallas kernels: 75.8 us -> 73.1 us  [per_device(): pl.pallas_call(functools.partial(kernel, dims), out_shape=(jax.ShapeDtype...]
    pallas_call x0 -> x1, Pallas kernels: none -> 2.24 us  [per_device(): pl.pallas_call(store, out_shape=tuple((jax.ShapeDtypeStruct(a.shape, a.dt...]
where the time goes in v3:
time: 76.2 us; the launch traced here: 76 us
  Pallas kernels  75.4 us (99%)
    pallas_call x1, Pallas kernels, per_device(): pl.pallas_call(functools.partial(kernel, dims), out_shape=(jax.ShapeDtype...  73.1 us
    pallas_call x1, Pallas kernels, per_device(): pl.pallas_call(store, out_shape=tuple((jax.ShapeDtypeStruct(a.shape, a.dt...  2.24 us

profile of v3, /device:TPU:1, one launch (start us, length us, event | category | flops | bytes accessed | tf_op | source)
XLA Modules:
  0.0 76.0 jit_solution(7461256977891489252)
XLA Ops:
  0.6 73.1 %shard_map.112 = (bf16[384,2048]{1,0:T(8,128)(2,1)}, f32[3,32,128]{2,1,0:T(8,128)}, f32[32,128]{1,0:T(8,128)}) custom-call(bf16[384,2048]{1,0:T(8,128)(2,1)} %tok_hbm.1, f32[1,2048]{1,0:T(1,128)} %bitcast.8, bf16[3,32,128]{2,1,0:T(8,128)(2,1)} %bitcast.7, f32[3,1,32]{2,1,0:T(1,128)} %bitcast.9, bf16[32,128]{1,0:T(8,128)(2,1)} %ocodes.1, f32[1,32]{1,0:T(1,128)} %bitcast.11, ...), custom_call_target="tpu_custom_call" | custom-call | flops 4000000000 | bytes 6000000 | tf_op jit(solution)/shard_map/pallas_call | solution.py:526
  73.8 2.2 %shard_map.113 = (bf16[384,2048]{1,0:T(8,128)(2,1)}, f32[3,32,128]{2,1,0:T(8,128)}, f32[32,128]{1,0:T(8,128)}) custom-call(bf16[384,2048]{1,0:T(8,128)(2,1)} %get-tuple-element.9.refs_0_, f32[3,32,128]{2,1,0:T(8,128)} %get-tuple-element.10.refs_1_, f32[32,128]{1,0:T(8,128)} %get-tuple-element.11.refs_2_), custom_call_target="tpu_custom_call" | custom-call | tf_op jit(solution)/shard_map/pallas_call | solution.py:554

commit v4 on v3

--- a/solution.py
+++ b/solution.py
@@ -39,8 +39,8 @@
     dims,
     tok_hbm, gain, codes, scales, ocodes, oscales, maskb, counts, ups_hbm,
     mixed, gq, go,
-    tok, ups, bias, normed, ntr, utr, nts, uts, wbuf, wof, qd, kv, ebuf, pbuf, dsb, dqa, atts,
-    att_all, hgs, hgr, ogr, dd, g, rss, rsr, fin, zs, zr,
+    tok, ups, bias, normed, ntr, utr, nts, uts, wbuf, wof, qd, kv, ebuf, pbuf, dsb, atts,
+    att_all, mixv, hgs, hgr, ogr, dd, g, rss, rsr, fin, zs, zr,
     agz, agy, ags, halo, tsw, wos, wps, ats, hgm, dds, rsm, zsm, loc,
 ):
     ZH, Y, ZL, X = dims
@@ -119,7 +119,7 @@
     barrier = pltpu.get_barrier_semaphore()
     partners = [odev(owner(j)) for j in range(1, NOWN)]
     partners += [{"zh": zk(k)} for k in range(1, ZH)]
-    partners += [nxt, prv, ydev(2), ydev(-2), ydev(1), ydev(-1), sib]
+    partners += [nxt, prv, ydev(2), ydev(-2), ydev(1), ydev(-1)]
     for dev in partners:
         pl.semaphore_signal(barrier, inc=1, device_id=dev, device_id_type=MESH)
     load_tok = keep(tok_hbm, tok, 0)
@@ -303,30 +303,30 @@
         send(atts, att_all.at[:, lanes(own, HEAD)], ats, (j,), odev(owner(j)))
     keep_att = keep(atts, att_all.at[:, lanes(own, HEAD)], 3)
 
+    def to_neighbour(seg, j, value):
+        side = seg // 2
+        hgs[side, j] = value.astype(BF)
+        send(hgs.at[side, j], hgr.at[side, j], hgm, (side, j), prv if seg == 0 else nxt)
+
+    for seg in (0, 2):
+        to_neighbour(seg, 1, tn(pbuf[seg], qd[1]))
     for seg in (0, 2, 1):
         for b in range(NQ):
             rows = slice(b * BLK, (b + 1) * BLK)
             dp = nt(qd[1, rows, :], kv[seg, 1])
-            ds = (ebuf[seg, rows, :] * (dp - deltas[b]) * INV_ROOT).astype(BF)
-            dsb[seg, rows, :] = ds
-            term = nn(ds, kv[seg, 0])
-            if seg == 0:
-                dqa[rows, :] = term
-            else:
-                dqa[rows, :] += term
-        if seg == 1:
-            dd[0, :, W : 3 * HEAD] = dqa[...].astype(BF)
-            part = pl.ds(W, HEAD)
-            send(dd.at[0, :, part], dd.at[1, :, part], dds, (1,), sib)
-        dk = tn(dsb[seg], qd[0])
-        dv = tn(pbuf[seg], qd[1])
-        if seg == 1:
-            ogr[0] = dk
-            ogr[1] = dv
-        else:
-            hgs[seg // 2, 0] = dk.astype(BF)
-            hgs[seg // 2, 1] = dv.astype(BF)
-            send(hgs.at[seg // 2], hgr.at[seg // 2], hgm, (seg // 2,), prv if seg == 0 else nxt)
+            dsb[seg, rows, :] = (ebuf[seg, rows, :] * (dp - deltas[b]) * INV_ROOT).astype(BF)
+        if seg != 1:
+            to_neighbour(seg, 0, tn(dsb[seg], qd[0]))
+    for b in range(NQ):
+        rows = slice(b * BLK, (b + 1) * BLK)
+        total = nn(dsb[0, rows, :], kv[0, 0])
+        for seg in (1, 2):
+            total += nn(dsb[seg, rows, :], kv[seg, 0])
+        dd[0, rows, W : 3 * HEAD] = total.astype(BF)
+    part = pl.ds(W, HEAD)
+    send(dd.at[0, :, part], dd.at[1, :, part], dds, (1,), sib)
+    ogr[0] = tn(dsb[1], qd[0])
+    ogr[1] = tn(pbuf[1], qd[1])
 
     high = ZH * ROWS
 
@@ -413,7 +413,9 @@
         w = wof[z].reshape(n, NOWN * HEAD)
         for b in range(NQ):
             rows = slice(b * BLK, (b + 1) * BLK)
-            mixed[rows, z * n : (z + 1) * n] = nt(att_all[rows, :], w).astype(BF)
+            mixv[rows, z * n : (z + 1) * n] = nt(att_all[rows, :], w).astype(BF)
+        part = pl.ds(z * n, n)
+        locals_.append(keep(mixv.at[:, part], mixed.at[:, part], 4 + z))
 
     arrived(uts, tsw, (0,))
     arrived(nts, tsw, (1,))
@@ -423,7 +425,8 @@
     rs_step(1, 0)
     rs_terms(1, 1)
     for side in range(2):
-        arrived(hgr.at[side], hgm, (side,))
+        for j in range(2):
+            arrived(hgr.at[side, j], hgm, (side, j))
     for j in range(2):
         both = ogr[j] + hgr[0, j].astype(F32) + hgr[1, j].astype(F32)
         dd[0, :, j * HEAD : (j + 1) * HEAD] = both.astype(BF)
@@ -505,9 +508,9 @@
         ((3, T, T), F32),
         ((3, T, T), BF),
         ((3, T, T), BF),
-        ((T, HEAD), F32),
         ((T, HEAD), BF),
         ((T, NOWN * HEAD), BF),
+        ((T, D), BF),
         ((2, 2, T, HEAD), BF),
         ((2, 2, T, HEAD), BF),
         ((2, T, HEAD), F32),
@@ -521,7 +524,7 @@
     ]
     sems = [
         (2, 2, ZH), (2, 2, H, 2, 2), (2, 2, Y), (2, 2, 2), (2, 2), (2, NOWN), (2, NOWN), (2, NOWN),
-        (2, 2), (2, 3), (2, 2, 2, H, 2), (2, 2, ZH), (4,),
+        (2, 2, 2), (2, 3), (2, 2, 2, H, 2), (2, 2, ZH), (4 + ZH,),
     ]
     mixed, gq, go = pl.pallas_call(
         functools.partial(kernel, dims),
@@ -531,7 +534,7 @@
             jax.ShapeDtypeStruct((ROWS, HEAD), F32),
         ),
         in_specs=[far] + [vmem] * 7 + [far],
-        out_specs=(vmem,) * 3,
+        out_specs=(far, vmem, vmem),
         scratch_shapes=[pltpu.VMEM(s, t) for s, t in buffers]
         + [pltpu.SemaphoreType.DMA(s) for s in sems],
         compiler_params=pltpu.CompilerParams(

time: 76.2 us -> 75 us (0.984)
  Pallas kernels: 75.4 us -> 74.2 us
    pallas_call x1, Pallas kernels: 73.1 us -> 72 us  [per_device(): pl.pallas_call(functools.partial(kernel, dims), out_shape=(jax.ShapeDtype...]
where the time goes in v4:
time: 75 us; the launch traced here: 74.8 us
  Pallas kernels  74.2 us (99%)
    pallas_call x1, Pallas kernels, per_device(): pl.pallas_call(functools.partial(kernel, dims), out_shape=(jax.ShapeDtype...  72 us
    pallas_call x1, Pallas kernels, per_device(): pl.pallas_call(store, out_shape=tuple((jax.ShapeDtypeStruct(a.shape, a.dt...  2.24 us

profile of v4, /device:TPU:1, one launch (start us, length us, event | category | flops | bytes accessed | tf_op | source)
XLA Modules:
  0.0 74.8 jit_solution(10838600066202387782)
XLA Ops:
  0.6 72.0 %shard_map.112 = (bf16[384,2048]{1,0:T(8,128)(2,1)}, f32[3,32,128]{2,1,0:T(8,128)}, f32[32,128]{1,0:T(8,128)}) custom-call(bf16[384,2048]{1,0:T(8,128)(2,1)} %tok_hbm.1, f32[1,2048]{1,0:T(1,128)} %bitcast.8, bf16[3,32,128]{2,1,0:T(8,128)(2,1)} %bitcast.7, f32[3,1,32]{2,1,0:T(1,128)} %bitcast.9, bf16[32,128]{1,0:T(8,128)(2,1)} %ocodes.1, f32[1,32]{1,0:T(1,128)} %bitcast.11, ...), custom_call_target="tpu_custom_call" | custom-call | flops 4000000000 | bytes 6000000 | tf_op jit(solution)/shard_map/pallas_call | solution.py:529
  72.6 2.2 %shard_map.113 = (bf16[384,2048]{1,0:T(8,128)(2,1)}, f32[3,32,128]{2,1,0:T(8,128)}, f32[32,128]{1,0:T(8,128)}) custom-call(bf16[384,2048]{1,0:T(8,128)(2,1)} %get-tuple-element.9.refs_0_, f32[3,32,128]{2,1,0:T(8,128)} %get-tuple-element.10.refs_1_, f32[32,128]{1,0:T(8,128)} %get-tuple-element.11.refs_2_), custom_call_target="tpu_custom_call" | custom-call | tf_op jit(solution)/shard_map/pallas_call | solution.py:557

commit v5 on v4

--- a/solution.py
+++ b/solution.py
@@ -299,9 +299,6 @@
         deltas.append(jnp.sum(total * qd[1, rows, :].astype(F32), axis=-1, keepdims=True))
     dd[0, :, 3 * HEAD :] = atts[...]
     send(dd.at[0, :, pl.ds(3 * HEAD, HEAD)], dd.at[1, :, pl.ds(3 * HEAD, HEAD)], dds, (0,), sib)
-    for j in range(1, NOWN):
-        send(atts, att_all.at[:, lanes(own, HEAD)], ats, (j,), odev(owner(j)))
-    keep_att = keep(atts, att_all.at[:, lanes(own, HEAD)], 3)
 
     def to_neighbour(seg, j, value):
         side = seg // 2
@@ -310,6 +307,9 @@
 
     for seg in (0, 2):
         to_neighbour(seg, 1, tn(pbuf[seg], qd[1]))
+    for j in range(1, NOWN):
+        send(atts, att_all.at[:, lanes(own, HEAD)], ats, (j,), odev(owner(j)))
+    keep_att = keep(atts, att_all.at[:, lanes(own, HEAD)], 3)
     for seg in (0, 2, 1):
         for b in range(NQ):
             rows = slice(b * BLK, (b + 1) * BLK)

time: 75 us -> 75 us (level)
  no operation moved by 1% of the time
where the time goes in v5:
time: 75 us; the launch traced here: 74.8 us
  Pallas kernels  74.2 us (99%)
    pallas_call x1, Pallas kernels, per_device(): pl.pallas_call(functools.partial(kernel, dims), out_shape=(jax.ShapeDtype...  71.9 us
    pallas_call x1, Pallas kernels, per_device(): pl.pallas_call(store, out_shape=tuple((jax.ShapeDtypeStruct(a.shape, a.dt...  2.24 us

profile of v5, /device:TPU:1, one launch (start us, length us, event | category | flops | bytes accessed | tf_op | source)
XLA Modules:
  0.0 74.8 jit_solution(11788811721046057150)
XLA Ops:
  0.6 71.9 %shard_map.112 = (bf16[384,2048]{1,0:T(8,128)(2,1)}, f32[3,32,128]{2,1,0:T(8,128)}, f32[32,128]{1,0:T(8,128)}) custom-call(bf16[384,2048]{1,0:T(8,128)(2,1)} %tok_hbm.1, f32[1,2048]{1,0:T(1,128)} %bitcast.8, bf16[3,32,128]{2,1,0:T(8,128)(2,1)} %bitcast.7, f32[3,1,32]{2,1,0:T(1,128)} %bitcast.9, bf16[32,128]{1,0:T(8,128)(2,1)} %ocodes.1, f32[1,32]{1,0:T(1,128)} %bitcast.11, ...), custom_call_target="tpu_custom_call" | custom-call | flops 4000000000 | bytes 6000000 | tf_op jit(solution)/shard_map/pallas_call | solution.py:529
  72.6 2.2 %shard_map.113 = (bf16[384,2048]{1,0:T(8,128)(2,1)}, f32[3,32,128]{2,1,0:T(8,128)}, f32[32,128]{1,0:T(8,128)}) custom-call(bf16[384,2048]{1,0:T(8,128)(2,1)} %get-tuple-element.9.refs_0_, f32[3,32,128]{2,1,0:T(8,128)} %get-tuple-element.10.refs_1_, f32[32,128]{1,0:T(8,128)} %get-tuple-element.11.refs_2_), custom_call_target="tpu_custom_call" | custom-call | tf_op jit(solution)/shard_map/pallas_call | solution.py:557
